TPU v7x, 32 devices: a whole 2x2x4 slice. The times are simulated.
32 devices in a mesh: dp: 4 (over y, x), seq: 8 (over z, core).
Axes of the slice: x: 2, y: 2, z: 4, core: 2. Of those that a mesh axis runs over, the one named last changes fastest.
Arguments:
- layer_input: bfloat16 [4, 1024, 2048], P('dp', 'seq'), may hold values from -6 to 6
- segment_ids: int32 [4, 1024], P('dp'), may hold values from 0 to 7, never falling along the last dimension, each value on 1 to 512 neighbouring positions
- first_gain: bfloat16 [2048], P(('dp', 'seq')), may hold values from 0.5 to 1.5
- query_down: bfloat16 [2048, 1024], P(('dp', 'seq')), may hold values from -0.125 to 0.125
- query_gain: bfloat16 [1024], P(('dp', 'seq')), may hold values from 0.5 to 1.5
- query_up: bfloat16 [1024, 4096], P(('dp', 'seq')), may hold values from -0.1875 to 0.1875
- key_proj: bfloat16 [2048, 256], P(('dp', 'seq')), may hold values from -0.125 to 0.125
- value_proj: bfloat16 [2048, 256], P(('dp', 'seq')), may hold values from -0.125 to 0.125
- out_proj: bfloat16 [4096, 2048], P(('dp', 'seq')), may hold values from -0.75 to 0.75
- second_gain: bfloat16 [2048], P(('dp', 'seq')), may hold values from 0.5 to 1.5
- w_gate: bfloat16 [2048, 5632], P(None, 'seq'), may hold values from -0.125 to 0.125
- w_up: bfloat16 [2048, 5632], P(None, 'seq'), may hold values from -0.125 to 0.125
- w_down: bfloat16 [5632, 2048], P('seq'), may hold values from -0.078125 to 0.078125
- cotangent: bfloat16 [4, 1024, 2048], P('dp', 'seq'), may hold values from -6 to 6
Outputs:
- layer_out: float32 [4, 1024, 2048], P('dp', 'seq')
- d_input: float32 [4, 1024, 2048], P('dp', 'seq')
- d_first: float32 [2048], P(('dp', 'seq'))
- d_qdown: float32 [2048, 1024], P(('dp', 'seq'))
- d_qgain: float32 [1024], P(('dp', 'seq'))
- d_qup: float32 [1024, 4096], P(('dp', 'seq'))
- d_key: float32 [2048, 256], P(('dp', 'seq'))
- d_value: float32 [2048, 256], P(('dp', 'seq'))
- d_out: float32 [4096, 2048], P(('dp', 'seq'))
- d_second: float32 [2048], P(('dp', 'seq'))
- d_gate: float32 [2048, 5632], P(None, 'seq')
- d_up: float32 [2048, 5632], P(None, 'seq')
- d_down: float32 [5632, 2048], P('seq')
Inputs may be any that keep to these rules, and one draw needn't show every extreme that they name: `segment_ids`: along a row the numbers never fall; every number of a row holds 1 to 512 consecutive tokens, and one holds exactly 512.
All inputs are finite; a program needn't handle non-finite values.
Results may differ from a plain program's by a relative error of at most 0.015.
Values may be sent and summed in bfloat16 or wider, within the bound.
No kernel may reach another device: no remote copies, remote signals or barrier semaphores. Data moves between devices by JAX's collectives and lax.ppermute only.
A program may use at most 384 MiB of HBM per device.

v0:
```python
import jax
import jax.numpy as jnp
from jax import lax
from jax.sharding import PartitionSpec as P

HEADS = 16
HEAD = 256


epsilon = 1e-06
masked_value = -1e30


def norm_apply(data_rows, gain_vec):
    inverse_rms = lax.rsqrt(jnp.mean(data_rows * data_rows, -1, keepdims=True) + epsilon)
    return data_rows * inverse_rms * gain_vec


def rotate(data_rows, cosine_table, sine_table):
    half_size = data_rows.shape[-1] // 2
    turned = jnp.concatenate([-data_rows[..., half_size:], data_rows[..., :half_size]], -1)
    return data_rows * cosine_table + turned * sine_table


def angle_tables(positions, head_size):
    frequency = 10000.0 ** (-jnp.arange(0, head_size, 2).astype(jnp.float32) / head_size)
    angles = positions.astype(jnp.float32)[:, None] * frequency[None, :]
    angles = jnp.concatenate([angles, angles], -1)
    return (jnp.cos(angles), jnp.sin(angles))


def matmul(left_op, right_op):
    return jnp.dot(left_op, right_op, preferred_element_type=jnp.float32)


def dot_across(left_op, right_op):
    return lax.dot_general(
        left_op, right_op, (((0,), (0,)), ((), ())), preferred_element_type=jnp.float32
    )


def dot_transposed(left_op, right_op):
    return lax.dot_general(
        left_op, right_op, (((1,), (1,)), ((), ())), preferred_element_type=jnp.float32
    )


def gather_layer(
    first_gain, query_down, query_gain, query_up, key_proj, value_proj, out_proj, second_gain
):
    return (
        lax.all_gather(first_gain, ("dp", "seq"), axis=0, tiled=True),
        lax.all_gather(query_down, ("dp", "seq"), axis=0, tiled=True),
        lax.all_gather(query_gain, ("dp", "seq"), axis=0, tiled=True),
        lax.all_gather(query_up, ("dp", "seq"), axis=0, tiled=True),
        lax.all_gather(key_proj, ("dp", "seq"), axis=0, tiled=True),
        lax.all_gather(value_proj, ("dp", "seq"), axis=0, tiled=True),
        lax.all_gather(out_proj, ("dp", "seq"), axis=0, tiled=True),
        lax.all_gather(second_gain, ("dp", "seq"), axis=0, tiled=True),
    )


def front_pass(inputs, segment_row, weights_all, positions, cosine_table, sine_table):
    (
        gain_first,
        down_query,
        gain_query,
        up_query,
        key_weights,
        value_weights,
        out_weights,
        gain_second,
    ) = weights_all
    tok_rows = inputs.shape[0]
    normed_in = norm_apply(inputs, gain_first.astype(jnp.float32)).astype(jnp.bfloat16)
    query_low = matmul(normed_in, down_query)
    query_norm = norm_apply(query_low, gain_query.astype(jnp.float32)).astype(jnp.bfloat16)
    query_raw = matmul(query_norm, up_query).reshape(tok_rows, HEADS, HEAD)
    queries = rotate(query_raw, cosine_table[:, None, :], sine_table[:, None, :]).astype(
        jnp.bfloat16
    )
    key_own = rotate(matmul(normed_in, key_weights), cosine_table, sine_table).astype(jnp.bfloat16)
    value_own = matmul(normed_in, value_weights).astype(jnp.bfloat16)
    key_value = jnp.concatenate([key_own, value_own], -1)
    kv_all = lax.all_gather(key_value, "seq", axis=0, tiled=True)
    own_segments = lax.dynamic_slice_in_dim(segment_row, positions[0], tok_rows, 0)
    all_positions = jnp.arange(segment_row.shape[0], dtype=jnp.int32)
    allowed = (all_positions[None, :] <= positions[:, None]) & (
        segment_row[None, :] == own_segments[:, None]
    )
    logits = jnp.einsum(
        "thd,sd->ths", queries, kv_all[:, :HEAD], preferred_element_type=jnp.float32
    ) * HEAD ** (-0.5)
    masked = jnp.where(allowed[:, None, :], logits, masked_value)
    attention = jax.nn.softmax(masked, axis=-1)
    attended = jnp.einsum(
        "ths,sd->thd",
        attention.astype(jnp.bfloat16),
        kv_all[:, HEAD:],
        preferred_element_type=jnp.float32,
    )
    attended = attended.reshape(tok_rows, HEADS * HEAD).astype(jnp.bfloat16)
    mid_sum = inputs + matmul(attended, out_weights)
    normed_mid = norm_apply(mid_sum, gain_second.astype(jnp.float32)).astype(jnp.bfloat16)
    return (
        normed_in,
        query_low,
        query_norm,
        queries,
        kv_all,
        attention,
        attended,
        mid_sum,
        normed_mid,
    )


def feed_front(normed_mid, w_gate, w_up):
    normed_all = lax.all_gather(normed_mid, "seq", axis=0, tiled=True)
    return feed_local(normed_all, w_gate, w_up)


def feed_local(normed_rows_in, gate_weights, up_weights):
    gate_pre = matmul(normed_rows_in, gate_weights)
    up_pre = matmul(normed_rows_in, up_weights)
    hidden = (jax.nn.silu(gate_pre) * up_pre).astype(jnp.bfloat16)
    return (normed_rows_in, gate_pre, up_pre, hidden)


def gated_unit(gate_in, up_in):
    return jax.nn.silu(gate_in) * up_in


def local(
    layer_input,
    segment_ids,
    first_gain,
    query_down,
    query_gain,
    query_up,
    key_proj,
    value_proj,
    out_proj,
    second_gain,
    w_gate,
    w_up,
    w_down,
    cotangent,
):
    inputs = layer_input[0].astype(jnp.float32)
    segment_row = segment_ids[0]
    tok_rows = inputs.shape[0]
    positions = lax.axis_index("seq") * tok_rows + jnp.arange(tok_rows, dtype=jnp.int32)
    cosine_table, sine_table = angle_tables(positions, HEAD)
    weights_all = gather_layer(
        first_gain, query_down, query_gain, query_up, key_proj, value_proj, out_proj, second_gain
    )
    stored_front = front_pass(inputs, segment_row, weights_all, positions, cosine_table, sine_table)
    feed_state = feed_front(stored_front[8], w_gate, w_up)
    hidden_now = feed_state[3]
    branch_out = lax.psum_scatter(
        matmul(hidden_now, w_down), "seq", scatter_dimension=0, tiled=True
    )
    layer_out = stored_front[7] + branch_out
    weights_all = gather_layer(
        first_gain, query_down, query_gain, query_up, key_proj, value_proj, out_proj, second_gain
    )
    stored_front = front_pass(inputs, segment_row, weights_all, positions, cosine_table, sine_table)
    feed_state = feed_front(stored_front[8], w_gate, w_up)
    (
        gain_first,
        down_query,
        gain_query,
        up_query,
        key_weights,
        value_weights,
        out_weights,
        gain_second,
    ) = weights_all
    normed_in, query_low, query_norm, queries, kv_all, attention, attended, mid_sum, normed_mid = (
        stored_front
    )
    normed_all, gate_pre, up_pre, hidden = feed_state
    cot_rows = cotangent[0]
    piece_rows = lax.all_gather(cot_rows, "seq", axis=0, tiled=True)
    down_grad = dot_across(hidden, piece_rows)
    grad_hidden = dot_transposed(piece_rows, w_down)
    gated_value, gate_pull = jax.vjp(gated_unit, gate_pre, up_pre)
    gate_grad, up_grad = gate_pull(grad_hidden)
    gate_grad = gate_grad.astype(jnp.bfloat16)
    up_grad = up_grad.astype(jnp.bfloat16)
    gating_grad = dot_across(normed_all, gate_grad)
    upward_grad = dot_across(normed_all, up_grad)
    normed_grad = lax.psum_scatter(
        dot_transposed(gate_grad, w_gate) + dot_transposed(up_grad, w_up),
        "seq",
        scatter_dimension=0,
        tiled=True,
    )
    feed_grads = lax.psum((gating_grad, upward_grad, down_grad), "dp")
    norm_value, second_pull = jax.vjp(norm_apply, mid_sum, gain_second.astype(jnp.float32))
    mid_grad, second_grad = second_pull(normed_grad)
    mid_grad = mid_grad + cot_rows.astype(jnp.float32)
    attn_grad = mid_grad.astype(jnp.bfloat16)
    output_grad = dot_across(attended, attn_grad)
    context_grad = (
        dot_transposed(attn_grad, out_weights).astype(jnp.bfloat16).reshape(tok_rows, HEADS, HEAD)
    )
    key_all = kv_all[:, :HEAD]
    value_all = kv_all[:, HEAD:]
    scale_value = HEAD ** (-0.5)
    probs_grad = jnp.einsum(
        "thd,sd->ths", context_grad, value_all, preferred_element_type=jnp.float32
    )
    inner_sum = jnp.sum(attention * probs_grad, -1, keepdims=True)
    logit_grad = (attention * (probs_grad - inner_sum)).astype(jnp.bfloat16)
    queries_grad = (
        jnp.einsum("ths,sd->thd", logit_grad, key_all, preferred_element_type=jnp.float32)
        * scale_value
    )
    keys_grad = (
        jnp.einsum("ths,thd->sd", logit_grad, queries, preferred_element_type=jnp.float32)
        * scale_value
    )
    values_grad = jnp.einsum(
        "ths,thd->sd",
        attention.astype(jnp.bfloat16),
        context_grad,
        preferred_element_type=jnp.float32,
    )
    kv_grads = lax.psum_scatter(
        jnp.concatenate([keys_grad, values_grad], -1), "seq", scatter_dimension=0, tiled=True
    )
    key_grad = rotate(kv_grads[:, :HEAD], cosine_table, -sine_table).astype(jnp.bfloat16)
    value_grad = kv_grads[:, HEAD:].astype(jnp.bfloat16)
    query_grad = rotate(queries_grad, cosine_table[:, None, :], -sine_table[:, None, :])
    query_grad = query_grad.reshape(tok_rows, HEADS * HEAD).astype(jnp.bfloat16)
    lifted_grad = dot_across(query_norm, query_grad)
    compact_grad = dot_transposed(query_grad, up_query)
    query_value, query_pull = jax.vjp(norm_apply, query_low, gain_query.astype(jnp.float32))
    latent_grad, compact_gain = query_pull(compact_grad)
    latent_grad = latent_grad.astype(jnp.bfloat16)
    compress_grad = dot_across(normed_in, latent_grad)
    keymap_grad = dot_across(normed_in, key_grad)
    valuemap_grad = dot_across(normed_in, value_grad)
    entry_grad = (
        dot_transposed(latent_grad, down_query)
        + dot_transposed(key_grad, key_weights)
        + dot_transposed(value_grad, value_weights)
    )
    first_value, first_pull = jax.vjp(norm_apply, inputs, gain_first.astype(jnp.float32))
    inputs_grad, first_grad = first_pull(entry_grad)
    inputs_grad = inputs_grad + mid_grad
    layer_grads = (
        lax.psum_scatter(first_grad, ("dp", "seq"), scatter_dimension=0, tiled=True),
        lax.psum_scatter(compress_grad, ("dp", "seq"), scatter_dimension=0, tiled=True),
        lax.psum_scatter(compact_gain, ("dp", "seq"), scatter_dimension=0, tiled=True),
        lax.psum_scatter(lifted_grad, ("dp", "seq"), scatter_dimension=0, tiled=True),
        lax.psum_scatter(keymap_grad, ("dp", "seq"), scatter_dimension=0, tiled=True),
        lax.psum_scatter(valuemap_grad, ("dp", "seq"), scatter_dimension=0, tiled=True),
        lax.psum_scatter(output_grad, ("dp", "seq"), scatter_dimension=0, tiled=True),
        lax.psum_scatter(second_grad, ("dp", "seq"), scatter_dimension=0, tiled=True),
    )
    return (
        layer_out[None],
        inputs_grad[None],
        layer_grads[0],
        layer_grads[1],
        layer_grads[2],
        layer_grads[3],
        layer_grads[4],
        layer_grads[5],
        layer_grads[6],
        layer_grads[7],
        feed_grads[0],
        feed_grads[1],
        feed_grads[2],
    )


def solution(mesh):
    return jax.shard_map(
        local,
        mesh=mesh,
        in_specs=(
            P("dp", "seq", None),
            P("dp", None),
            P(("dp", "seq")),
            P(("dp", "seq"), None),
            P(("dp", "seq")),
            P(("dp", "seq"), None),
            P(("dp", "seq"), None),
            P(("dp", "seq"), None),
            P(("dp", "seq"), None),
            P(("dp", "seq")),
            P(None, "seq"),
            P(None, "seq"),
            P("seq", None),
            P("dp", "seq", None),
        ),
        out_specs=(
            P("dp", "seq", None),
            P("dp", "seq", None),
            P(("dp", "seq")),
            P(("dp", "seq"), None),
            P(("dp", "seq")),
            P(("dp", "seq"), None),
            P(("dp", "seq"), None),
            P(("dp", "seq"), None),
            P(("dp", "seq"), None),
            P(("dp", "seq")),
            P(None, "seq"),
            P(None, "seq"),
            P("seq", None),
        ),
        check_vma=False,
    )
```

profile of v0, /device:TPU:0, one launch (start us, length us, event | category | flops | bytes accessed | tf_op | source)
XLA Modules:
  0.0 2094.7 jit_solution(2040857871681767819)
XLA Ops:
  12.6 42.2 %all-reduce.8 = (bf16[2048]{0:T(1024)(128)(2,1)S(1)}, bf16[1024]{0:T(1024)(128)(2,1)}, bf16[2048]{0:T(1024)(128)(2,1)}) all-reduce(bf16[2048]{0:T(1024)(128)(2,1)S(1)} %dynamic-update-slice, bf16[1024]{0:T(1024)(128)(2,1)S(1)} %dynamic-update-slice.1, bf16[2048]{0:T(1024)(128)(2,1)S(1)} %dynamic-update-slice.2), channel_id=1, replica_groups=mesh['dp'=4,'seq'=8] {'dp','seq'}, use_global_device_ids=true, to_apply=%add | all-reduce | flops 5120 | bytes 20480
  56.7 10.9 all-gather.14.cloned.1.call-done
  70.6 52.8 %all-gather.16.cloned.1.call-done = bf16[2048,256]{1,0:T(8,128)(2,1)} async-done(((bf16[64,256]{1,0:T(8,128)(2,1)}), bf16[2048,256]{1,0:T(8,128)(2,1)}) %all-gather.16.cloned.1.call-update) | async-done | bytes 1048592 | tf_op jit(solution)/shard_map/all_gather | solution.py:57
  133.7 53.8 %all-gather.10.cloned.1.call-done = bf16[2048,1024]{1,0:T(8,128)(2,1)} async-done(((bf16[64,1024]{1,0:T(8,128)(2,1)}), bf16[2048,1024]{1,0:T(8,128)(2,1)}) %all-gather.10.cloned.1.call-update) | async-done | bytes 4194320 | tf_op jit(solution)/shard_map/all_gather | solution.py:53
  191.3 75.1 %all-gather.12.cloned.1.call-done = bf16[1024,4096]{1,0:T(8,128)(2,1)} async-done(((bf16[32,4096]{1,0:T(8,128)(2,1)}), bf16[1024,4096]{1,0:T(8,128)(2,1)}) %all-gather.12.cloned.1.call-update) | async-done | bytes 8388624 | tf_op jit(solution)/shard_map/all_gather | solution.py:55
  275.7 13.5 all-gather.18.cloned.1.call-done
  305.6 100.9 %all-gather.20.cloned.1.call-done = bf16[4096,2048]{1,0:T(8,128)(2,1)} async-done(((bf16[128,2048]{1,0:T(8,128)(2,1)}), bf16[4096,2048]{1,0:T(8,128)(2,1)}) %all-gather.20.cloned.1.call-update) | async-done | bytes 16777232 | tf_op jit(solution)/shard_map/all_gather | solution.py:58
  406.5 8.5 multiply_reduce_fusion.3
  417.8 44.7 %all-gather.22.cloned.1.call-done = bf16[1024,2048]{1,0:T(8,128)(2,1)} async-done(((bf16[128,2048]{1,0:T(8,128)(2,1)}), bf16[1024,2048]{1,0:T(8,128)(2,1)}) %all-gather.22.cloned.1.call-update) | async-done | bytes 4194320 | tf_op jit(solution)/shard_map/all_gather | solution.py:119
  475.3 34.8 %all-gather.24.cloned.1.call-done = bf16[1,1024,2048]{2,1,0:T(8,128)(2,1)} async-done(((bf16[1,128,2048]{2,1,0:T(8,128)(2,1)}), bf16[1,1024,2048]{2,1,0:T(8,128)(2,1)}) %all-gather.24.cloned.1.call-update) | async-done | bytes 4194320 | tf_op jit(solution)/shard_map/all_gather | solution.py:185
  510.0 8.9 multiply_convert_fusion.1
  535.8 81.1 %reduce-scatter.11.cloned.1.call-done = f32[128,2048]{1,0:T(8,128)} async-done(((f32[1024,2048]{1,0:T(8,128)}), f32[128,2048]{1,0:T(8,128)}) %reduce-scatter.11.cloned.1.call-update) | async-done | bytes 1048592 | tf_op jit(solution)/shard_map/reduce_scatter | solution.py:194
  619.0 88.1 %reduce-scatter.9.cloned.1.call-done = f32[128,2048]{1,0:T(8,128)} async-done(((f32[1024,2048]{1,0:T(8,128)}), f32[128,2048]{1,0:T(8,128)}) %reduce-scatter.9.cloned.1.call-update) | async-done | bytes 1048592 | tf_op jit(solution)/shard_map/reduce_scatter | solution.py:161
  709.9 11.4 convolution_convert_fusion
  760.9 15.6 reduce-scatter.13.cloned.1.call-done
  802.0 8.5 fusion.63
  811.7 13.8 fusion.45
  832.0 39.1 %all-reduce.6 = (f32[2048]{0:T(1024)S(1)}, f32[1024]{0:T(1024)S(1)}, f32[2048]{0:T(1024)S(1)}) all-reduce(f32[2048]{0:T(1024)S(1)} %get-tuple-element.15, f32[1024]{0:T(1024)S(1)} %get-tuple-element.17, f32[2048]{0:T(1024)S(1)} %copy-done.21), channel_id=6, replica_groups=mesh['dp'=4,'seq'=8] {'dp','seq'}, use_global_device_ids=true, to_apply=%region_13.14.clone | all-reduce | flops 5120 | bytes 40960
  875.4 223.5 %all-reduce.11.cloned.1.call-done = (f32[2048,704]{0,1:T(8,128)}, f32[2048,704]{0,1:T(8,128)}, f32[704,2048]{1,0:T(8,128)}) async-done(((f32[2048,704]{0,1:T(8,128)}, f32[2048,704]{0,1:T(8,128)}, f32[704,2048]{1,0:T(8,128)}), (f32[2048,704]{0,1:T(8,128)}, f32[2048,704]{0,1:T(8,128)}, f32[704,2048]{1,0:T(8,128)})) %all-reduce.11.cloned.1.call-update) | async-done | bytes 17301520 | tf_op jit(solution)/shard_map/psum | solution.py:200
  1098.9 140.7 %reduce-scatter.19.cloned.1.call-done = f32[64,256]{1,0:T(8,128)} async-done(((f32[2048,256]{1,0:T(8,128)}), f32[64,256]{1,0:T(8,128)}) %reduce-scatter.19.cloned.1.call-update) | async-done | bytes 65552 | tf_op jit(solution)/shard_map/reduce_scatter | solution.py:259
  1239.6 136.2 %reduce-scatter.21.cloned.1.call-done = f32[64,256]{1,0:T(8,128)} async-done(((f32[2048,256]{1,0:T(8,128)}), f32[64,256]{1,0:T(8,128)}) %reduce-scatter.21.cloned.1.call-update) | async-done | bytes 65552 | tf_op jit(solution)/shard_map/reduce_scatter | solution.py:260
  1375.8 151.0 %reduce-scatter.15.cloned.1.call-done = f32[64,1024]{1,0:T(8,128)} async-done(((f32[2048,1024]{1,0:T(8,128)}), f32[64,1024]{1,0:T(8,128)}) %reduce-scatter.15.cloned.1.call-update) | async-done | bytes 262160 | tf_op jit(solution)/shard_map/reduce_scatter | solution.py:256
  1526.9 187.1 %reduce-scatter.17.cloned.1.call-done = f32[32,4096]{1,0:T(8,128)} async-done(((f32[1024,4096]{1,0:T(8,128)}), f32[32,4096]{1,0:T(8,128)}) %reduce-scatter.17.cloned.1.call-update) | async-done | bytes 524304 | tf_op jit(solution)/shard_map/reduce_scatter | solution.py:258
  1713.9 361.5 %reduce-scatter.23.cloned.1.call-done = f32[128,2048]{1,0:T(8,128)} async-done(((f32[4096,2048]{1,0:T(8,128)}), f32[128,2048]{1,0:T(8,128)}) %reduce-scatter.23.cloned.1.call-update) | async-done | bytes 1048592 | tf_op jit(solution)/shard_map/reduce_scatter | solution.py:261
  (189 shorter events, 176.2 us)
Async XLA Ops:
  7.2 502.8 %copy-start = (bf16[704,2048]{1,0:T(8,128)(2,1)S(1)}, bf16[704,2048]{1,0:T(8,128)(2,1)}, u32[]{:S(2)}) copy-start(bf16[704,2048]{1,0:T(8,128)(2,1)} %param.26) | copy-start | bytes 8650756
  7.2 180.4 %copy-start.2 = (bf16[1,128,2048]{2,1,0:T(8,128)(2,1)S(1)}, bf16[1,128,2048]{2,1,0:T(8,128)(2,1)}, u32[]{:S(2)}) copy-start(bf16[1,128,2048]{2,1,0:T(8,128)(2,1)} %param.14) | copy-start | bytes 1572868
  7.2 60.4 %all-gather.14.cloned.1.call-start = ((), (), s32[]{:S(2)}) async-start(), calls=%async_computation.10 | async-start | bytes 1081344 | tf_op jit(solution)/shard_map/all_gather | solution.py:56
  7.9 115.4 %all-gather.16.cloned.1.call-start = ((), (), s32[]{:S(2)}) async-start(), calls=%async_computation.11 | async-start | bytes 1081344 | tf_op jit(solution)/shard_map/all_gather | solution.py:57
  8.7 178.9 %all-gather.10.cloned.1.call-start = ((), (), s32[]{:S(2)}) async-start(), calls=%async_computation.8 | async-start | bytes 4325376 | tf_op jit(solution)/shard_map/all_gather | solution.py:53
  9.4 256.9 %all-gather.12.cloned.1.call-start = ((), (), s32[]{:S(2)}) async-start(), calls=%async_computation.9 | async-start | bytes 8650752 | tf_op jit(solution)/shard_map/all_gather | solution.py:55
  10.0 279.1 %all-gather.18.cloned.1.call-start = ((), (), s32[]{:S(2)}) async-start(), calls=%async_computation.12 | async-start | bytes 1179648 | tf_op jit(solution)/shard_map/all_gather | solution.py:85
  125.8 280.7 %all-gather.20.cloned.1.call-start = ((), (), s32[]{:S(2)}) async-start(), calls=%async_computation.13 | async-start | bytes 17301504 | tf_op jit(solution)/shard_map/all_gather | solution.py:58
  126.4 336.1 %all-gather.22.cloned.1.call-start = ((), (), s32[]{:S(2)}) async-start(), calls=%async_computation.14 | async-start | bytes 4718592 | tf_op jit(solution)/shard_map/all_gather | solution.py:119
  191.3 82.1 %copy-start.26 = (f32[128]{0:T(128)}, f32[128]{0:T(128)S(1)}, u32[]{:S(2)}) copy-start(f32[128]{0:T(128)S(1)} %get-tuple-element.46) | copy-start | bytes 1540
  191.3 82.1 %copy-start.22 = (f32[128]{0:T(128)}, f32[128]{0:T(128)S(1)}, u32[]{:S(2)}) copy-start(f32[128]{0:T(128)S(1)} %fusion.58) | copy-start | bytes 1540
  417.0 93.0 %all-gather.24.cloned.1.call-start = ((), (), s32[]{:S(2)}) async-start(), calls=%async_computation.23 | async-start | bytes 4718592 | tf_op jit(solution)/shard_map/all_gather | solution.py:185
  417.8 199.2 %reduce-scatter.11.cloned.1.call-start = ((), (), s32[]{:S(2)}) async-start(), calls=%async_computation.16 | async-start | bytes 9437184 | tf_op jit(solution)/shard_map/reduce_scatter | solution.py:194
  528.5 178.6 %reduce-scatter.9.cloned.1.call-start = ((), (), s32[]{:S(2)}) async-start(), calls=%async_computation.15 | async-start | bytes 9437184 | tf_op jit(solution)/shard_map/reduce_scatter | solution.py:161
  535.6 81.4 %copy-start.4 = (f32[128,2048]{1,0:T(8,128)S(1)}, f32[128,2048]{1,0:T(8,128)}, u32[]{:S(2)}) copy-start(f32[128,2048]{1,0:T(8,128)} %copy-done.3) | copy-start | bytes 3145732
  535.6 171.5 %copy-start.10 = (bf16[1,128,2048]{2,1,0:T(8,128)(2,1)S(1)}, bf16[1,128,2048]{2,1,0:T(8,128)(2,1)}, u32[]{:S(2)}) copy-start(bf16[1,128,2048]{2,1,0:T(8,128)(2,1)} %param.27) | copy-start | bytes 1572868
  535.6 240.9 %reduce-scatter.13.cloned.1.call-start = ((), (), s32[]{:S(2)}) async-start(), calls=%async_computation.17 | async-start | bytes 2359296 | tf_op jit(solution)/shard_map/reduce_scatter | solution.py:231
  742.2 356.7 %all-reduce.11.cloned.1.call-start = ((), (), s32[]{:S(2)}) async-start(), calls=%async_computation.24 | async-start | bytes 34603008 | tf_op jit(solution)/shard_map/psum | solution.py:200
  760.9 478.7 %reduce-scatter.19.cloned.1.call-start = ((), (), s32[]{:S(2)}) async-start(), calls=%async_computation.20 | async-start | bytes 2162688 | tf_op jit(solution)/shard_map/reduce_scatter | solution.py:259
  780.7 595.1 %reduce-scatter.21.cloned.1.call-start = ((), (), s32[]{:S(2)}) async-start(), calls=%async_computation.21 | async-start | bytes 2162688 | tf_op jit(solution)/shard_map/reduce_scatter | solution.py:260
  782.7 744.2 %reduce-scatter.15.cloned.1.call-start = ((), (), s32[]{:S(2)}) async-start(), calls=%async_computation.18 | async-start | bytes 8650752 | tf_op jit(solution)/shard_map/reduce_scatter | solution.py:256
  801.7 912.3 %reduce-scatter.17.cloned.1.call-start = ((), (), s32[]{:S(2)}) async-start(), calls=%async_computation.19 | async-start | bytes 17301504 | tf_op jit(solution)/shard_map/reduce_scatter | solution.py:258
  810.5 1265.0 %reduce-scatter.23.cloned.1.call-start = ((), (), s32[]{:S(2)}) async-start(), calls=%async_computation.22 | async-start | bytes 34603008 | tf_op jit(solution)/shard_map/reduce_scatter | solution.py:261
  829.3 43.6 %copy-start.25 = (f32[128]{0:T(128)S(1)}, f32[128]{0:T(128)}, u32[]{:S(2)}) copy-start(f32[128]{0:T(128)} %copy-done.24) | copy-start | bytes 1540
  (33 other events, 144.4 us)
Sparse Core Ops, SparseCore 0:
  11.0 56.5 all-gather.13
  70.6 52.7 all-gather.15
  126.4 61.1 all-gather.9
  190.4 75.9 all-gather.11
  268.4 20.6 all-gather.17
  292.0 114.5 all-gather.19
  417.2 45.3 all-gather.21
  464.1 45.8 all-gather.23
  528.6 88.3 reduce-scatter.10
  619.1 87.9 reduce-scatter.8
  742.3 34.1 reduce-scatter.12
  780.9 317.9 all-reduce.10
  1101.7 137.8 reduce-scatter.18
  1242.4 133.4 reduce-scatter.20
  1378.5 148.2 reduce-scatter.14
  1529.6 184.3 reduce-scatter.16
  1716.7 358.7 reduce-scatter.22
where the time goes:
time: 2100 us; the launch traced here: 2090 us
  waiting for transfers between devices  1780 us (85%)
  matrix products  163 us (8%)
  blocking collectives  81.3 us (4%)
  local copies, waits for them, and re-layouts  32.5 us (2%)
  other arithmetic  25.9 us (1%)
    reduce_scatter x1, waiting for transfers between devices, local(): lax.psum_scatter(output_grad, ('dp', 'seq'), scatter_dimension=0, tiled=T...  362 us
    psum x1, waiting for transfers between devices, local(): feed_grads = lax.psum((gating_grad, upward_grad, down_grad), 'dp')  223 us
    reduce_scatter x1, waiting for transfers between devices, local(): lax.psum_scatter(lifted_grad, ('dp', 'seq'), scatter_dimension=0, tiled=T...  187 us
    reduce_scatter x1, waiting for transfers between devices, local(): lax.psum_scatter(compress_grad, ('dp', 'seq'), scatter_dimension=0, tiled...  151 us
    reduce_scatter x1, waiting for transfers between devices, local(): lax.psum_scatter(keymap_grad, ('dp', 'seq'), scatter_dimension=0, tiled=T...  141 us
    reduce_scatter x1, waiting for transfers between devices, local(): lax.psum_scatter(valuemap_grad, ('dp', 'seq'), scatter_dimension=0, tiled...  136 us
    all_gather x1, waiting for transfers between devices, gather_layer(): lax.all_gather(out_proj, ('dp', 'seq'), axis=0, tiled=True)  101 us
    reduce_scatter x1, waiting for transfers between devices, local(): lax.psum_scatter(matmul(hidden_now, w_down), 'seq', scatter_dimension=0,...  88.1 us
  transfers between devices with their start and end apart: 17, of which 17 were waited for; matrix products, arithmetic and copies ran while one was open for 7% of the time, Pallas kernels for 0%

commit v1 on v0

--- a/solution.py
+++ b/solution.py
@@ -1,3 +1,5 @@
+import functools
+
 import jax
 import jax.numpy as jnp
 from jax import lax
@@ -131,7 +133,7 @@
     return jax.nn.silu(gate_in) * up_in
 
 
-def local(
+def local_tokens(
     layer_input,
     segment_ids,
     first_gain,
@@ -278,7 +280,297 @@
     )
 
 
+def local_heads(
+    row_count,
+    seq_count,
+    layer_input,
+    segment_ids,
+    first_gain,
+    query_down,
+    query_gain,
+    query_up,
+    key_proj,
+    value_proj,
+    out_proj,
+    second_gain,
+    w_gate,
+    w_up,
+    w_down,
+    cotangent,
+):
+    f32, bf16 = jnp.float32, jnp.bfloat16
+    seq_at = lax.axis_index("seq")
+    core_at = lax.rem(seq_at, 2)
+    swap = [(i, i ^ 1) for i in range(seq_count)]
+    own_rows = layer_input.shape[1]
+    length = own_rows * seq_count
+    width = layer_input.shape[2]
+    low_width = query_down.shape[1]
+    down_rows = query_down.shape[0]
+    up_rows = query_up.shape[0]
+    out_rows = out_proj.shape[0]
+    half_count = row_count // 2
+    chips = seq_count // 2
+    own_low = low_width // seq_count
+    low_part = own_low // row_count
+    kv_parts = seq_count // 2
+    kv_rows = length // kv_parts
+    kv_at = lax.rem(seq_at, kv_parts)
+    is_key = seq_at < kv_parts
+    spare = 8
+    own_heads = half_count
+
+    gains = jnp.zeros((spare, own_low + HEAD), bf16)
+    gains = gains.at[0, :down_rows].set(first_gain)
+    gains = gains.at[1, :down_rows].set(second_gain)
+    gains = gains.at[2, :up_rows].set(query_gain)
+    low_cols = query_down.reshape(down_rows, row_count, seq_count, low_part)
+    low_cols = low_cols.transpose(2, 0, 1, 3).reshape(seq_count, down_rows, own_low)
+    kv_cols = jnp.stack([key_proj] * kv_parts + [value_proj] * kv_parts)
+    sent = jnp.concatenate([low_cols, kv_cols], -1)
+    sent = jnp.concatenate(
+        [sent, jnp.broadcast_to(gains[None], (seq_count, spare, own_low + HEAD))], 1
+    )
+    sent = sent.reshape(seq_count * (down_rows + spare), own_low + HEAD)
+    sent = lax.all_to_all(sent, "seq", 0, 0, tiled=True)
+    entry_all = lax.all_gather(sent, "dp", axis=0, tiled=True)
+    entry_all = entry_all.reshape(row_count * seq_count, down_rows + spare, own_low + HEAD)
+    entry_weights = entry_all[:, :down_rows].reshape(width, own_low + HEAD)
+    gain_first = entry_all[:, down_rows, :down_rows].reshape(width).astype(f32)
+    gain_second = entry_all[:, down_rows + 1, :down_rows].reshape(width).astype(f32)
+    gain_query = entry_all[:, down_rows + 2, :up_rows].reshape(row_count, seq_count, low_part)
+    gain_query = gain_query.transpose(1, 0, 2).reshape(low_width).astype(f32)
+
+    inputs_all = lax.all_gather(layer_input[0], "seq", axis=0, tiled=True)
+
+    up_sent = query_up.reshape(up_rows, 2, half_count, chips, HEAD).transpose(3, 1, 0, 2, 4)
+    up_sent = up_sent.reshape(seq_count * up_rows, own_heads * HEAD)
+    up_mine = lax.all_to_all(up_sent, "seq", 0, 0, tiled=True)
+    up_mine = lax.all_gather(up_mine, "dp", axis=0, tiled=True)
+    up_mine = up_mine.reshape(row_count, seq_count, low_part, own_heads * HEAD)
+    up_mine = up_mine.transpose(1, 0, 2, 3).reshape(low_width, own_heads * HEAD)
+
+    out_all = lax.all_gather(out_proj, "dp", axis=0, tiled=False)
+    out_kept = lax.dynamic_slice_in_dim(out_all, core_at * half_count, half_count, 0)
+    out_given = lax.dynamic_slice_in_dim(out_all, (1 - core_at) * half_count, half_count, 0)
+    out_got = lax.ppermute(out_given, "seq", swap)
+    out_mine = jnp.where(
+        core_at == 0,
+        jnp.stack([out_kept, out_got], 1),
+        jnp.stack([out_got, out_kept], 1),
+    ).reshape(own_heads * HEAD, width)
+
+    cot_rows = cotangent[0]
+    cot_all = lax.all_gather(cot_rows, "seq", axis=0, tiled=True)
+
+    positions = jnp.arange(length, dtype=jnp.int32)
+    cosine_table, sine_table = angle_tables(positions, HEAD)
+
+    inputs_wide = inputs_all.astype(f32)
+    entry_scale = lax.rsqrt(jnp.mean(inputs_wide * inputs_wide, -1, keepdims=True) + epsilon)
+    normed_in = (inputs_wide * entry_scale * gain_first).astype(bf16)
+    low_own = matmul(normed_in, entry_weights)
+    kv_own = lax.dynamic_slice_in_dim(low_own[:, own_low:], kv_at * kv_rows, kv_rows, 0)
+    kv_cos = lax.dynamic_slice_in_dim(cosine_table, kv_at * kv_rows, kv_rows, 0)
+    kv_sin = lax.dynamic_slice_in_dim(sine_table, kv_at * kv_rows, kv_rows, 0)
+    kv_own = jnp.where(is_key, rotate(kv_own, kv_cos, kv_sin), kv_own).astype(bf16)
+    half_head = HEAD // 2
+    low_sent = jnp.concatenate(
+        [low_own[:, :own_low].astype(bf16), kv_own[:, :half_head], kv_own[:, half_head:]], 0
+    )
+    low_all = lax.all_gather(low_sent, "seq", axis=0, tiled=False)
+    query_low = low_all[:, :length].transpose(1, 0, 2).reshape(length, low_width).astype(f32)
+    kv_all = jnp.concatenate(
+        [low_all[:, length : length + kv_rows], low_all[:, length + kv_rows :]], -1
+    )
+    key_all = kv_all[:kv_parts].reshape(length, HEAD)
+    value_all = kv_all[kv_parts:].reshape(length, HEAD)
+
+    query_scale = lax.rsqrt(jnp.mean(query_low * query_low, -1, keepdims=True) + epsilon)
+    query_norm = (query_low * query_scale * gain_query).astype(bf16)
+    query_raw = matmul(query_norm, up_mine).reshape(length, own_heads, HEAD)
+    queries = rotate(query_raw, cosine_table[:, None, :], sine_table[:, None, :]).astype(bf16)
+    queries = queries.transpose(1, 0, 2)
+    segment_row = segment_ids[0]
+    allowed = (positions[None, :] <= positions[:, None]) & (
+        segment_row[None, :] == segment_row[:, None]
+    )
+    scale_value = HEAD ** (-0.5)
+    logits = (
+        jnp.einsum("htd,sd->hts", queries, key_all, preferred_element_type=f32) * scale_value
+    )
+    masked = jnp.where(allowed[None], logits, masked_value)
+    attention = jax.nn.softmax(masked, axis=-1)
+    attention_low = attention.astype(bf16)
+    attended = jnp.einsum("hts,sd->htd", attention_low, value_all, preferred_element_type=f32)
+    attended = attended.astype(bf16).transpose(1, 0, 2).reshape(length, own_heads * HEAD)
+    mixed = matmul(attended, out_mine).astype(bf16)
+    mixed = lax.psum_scatter(mixed, "seq", scatter_dimension=0, tiled=True).astype(f32)
+    mid_sum = layer_input[0].astype(f32) + mixed
+    mid_scale = lax.rsqrt(jnp.mean(mid_sum * mid_sum, -1, keepdims=True) + epsilon)
+    mid_unit = mid_sum * mid_scale
+    normed_mid = (mid_unit * gain_second).astype(bf16)
+
+    normed_all = lax.all_gather(normed_mid, "seq", axis=0, tiled=True)
+    grad_hidden = dot_transposed(cot_all, w_down)
+    gate_pre = matmul(normed_all, w_gate)
+    up_pre = matmul(normed_all, w_up)
+    hidden = gated_unit(gate_pre, up_pre)
+    gated_value, gate_pull = jax.vjp(gated_unit, gate_pre, up_pre)
+    hidden = gated_value.astype(bf16)
+    gate_grad, up_grad = gate_pull(grad_hidden)
+    gate_grad = gate_grad.astype(bf16)
+    up_grad = up_grad.astype(bf16)
+    normed_grad = dot_transposed(gate_grad, w_gate) + dot_transposed(up_grad, w_up)
+    normed_grad = lax.psum_scatter(
+        normed_grad.astype(bf16), "seq", scatter_dimension=0, tiled=True
+    ).astype(f32)
+    down_grad = dot_across(hidden, cot_all).astype(bf16)
+    gating_grad = dot_across(normed_all, gate_grad).astype(bf16)
+    upward_grad = dot_across(normed_all, up_grad).astype(bf16)
+    feed_grads = lax.psum((gating_grad, upward_grad, down_grad), "dp")
+    branch_out = lax.psum_scatter(
+        matmul(hidden, w_down).astype(bf16), "seq", scatter_dimension=0, tiled=True
+    )
+    layer_out = mid_sum + branch_out.astype(f32)
+
+    second_grad = jnp.sum(normed_grad * mid_unit, 0)
+    scaled_grad = normed_grad * gain_second
+    mid_grad = mid_scale * (
+        scaled_grad - mid_unit * jnp.mean(scaled_grad * mid_unit, -1, keepdims=True)
+    )
+    mid_grad = mid_grad + cot_rows.astype(f32)
+    attn_grad = lax.all_gather(mid_grad.astype(bf16), "seq", axis=0, tiled=True)
+
+    context_grad = dot_transposed(attn_grad, out_mine).astype(bf16)
+    context_grad = context_grad.reshape(length, own_heads, HEAD).transpose(1, 0, 2)
+    probs_grad = jnp.einsum("htd,sd->hts", context_grad, value_all, preferred_element_type=f32)
+    inner_sum = jnp.sum(attention * probs_grad, -1, keepdims=True)
+    logit_grad = (attention * (probs_grad - inner_sum)).astype(bf16)
+    queries_grad = (
+        jnp.einsum("hts,sd->htd", logit_grad, key_all, preferred_element_type=f32) * scale_value
+    )
+    keys_grad = (
+        jnp.einsum("hts,htd->sd", logit_grad, queries, preferred_element_type=f32) * scale_value
+    )
+    values_grad = jnp.einsum(
+        "hts,htd->sd", attention_low, context_grad, preferred_element_type=f32
+    )
+    query_grad = rotate(queries_grad, cosine_table, -sine_table).astype(bf16)
+    query_grad = query_grad.transpose(1, 0, 2).reshape(length, own_heads * HEAD)
+    compact_grad = dot_transposed(query_grad, up_mine)
+    query_unit = query_low * query_scale
+    compact_mean = jnp.sum(compact_grad * gain_query * query_unit, -1) / low_width
+    mean_rows = compact_mean.reshape(length // own_low, own_low)
+    compact_sent = compact_grad.astype(bf16).reshape(length, seq_count, own_low).transpose(1, 0, 2)
+    kv_sent = jnp.concatenate([keys_grad, values_grad], 0).astype(bf16)
+    kv_sent = kv_sent.reshape(seq_count, kv_rows, HEAD)
+    mean_high = mean_rows.astype(bf16)
+    mean_low = (mean_rows - mean_high.astype(f32)).astype(bf16)
+    means = jnp.broadcast_to(
+        jnp.concatenate([mean_high, mean_low], 0)[None],
+        (seq_count, 2 * mean_rows.shape[0], own_low),
+    )
+    back_sent = jnp.concatenate(
+        [compact_sent, kv_sent[:, :, :half_head], kv_sent[:, :, half_head:], means], 1
+    )
+    back = lax.psum_scatter(back_sent, "seq", scatter_dimension=0, tiled=False).astype(f32)
+
+    output_grad = dot_across(attended, attn_grad).astype(bf16)
+    output_grad = output_grad.reshape(own_heads, 2, out_rows, width)
+    grad_kept = lax.dynamic_index_in_dim(output_grad, core_at, 1, False)
+    grad_given = lax.dynamic_index_in_dim(output_grad, 1 - core_at, 1, False)
+    grad_got = lax.ppermute(grad_given, "seq", swap)
+    output_grad = jnp.where(
+        core_at == 0,
+        jnp.concatenate([grad_kept, grad_got], 0),
+        jnp.concatenate([grad_got, grad_kept], 0),
+    )
+    output_grad = lax.psum_scatter(output_grad, "dp", scatter_dimension=0, tiled=False)
+
+    lifted_grad = dot_across(query_norm, query_grad).astype(bf16)
+    lifted_grad = lifted_grad.reshape(seq_count, row_count, up_rows, own_heads * HEAD)
+    lifted_grad = lifted_grad.transpose(1, 0, 2, 3)
+    lifted_grad = lifted_grad.reshape(row_count * seq_count * up_rows, own_heads * HEAD)
+    lifted_grad = lax.psum_scatter(lifted_grad, "dp", scatter_dimension=0, tiled=True)
+    lifted_grad = lax.all_to_all(lifted_grad, "seq", 0, 0, tiled=True)
+    lifted_grad = lifted_grad.reshape(chips, 2, up_rows, half_count, HEAD)
+    lifted_grad = lifted_grad.transpose(2, 1, 3, 0, 4).reshape(up_rows, HEADS * HEAD)
+
+    compact_own = back[:length]
+    kv_back = jnp.concatenate(
+        [back[length : length + kv_rows], back[length + kv_rows : length + 2 * kv_rows]], -1
+    )
+    mean_back = back[length + 2 * kv_rows :].reshape(2, length).sum(0)[:, None]
+    low_at = seq_at * own_low
+    unit_own = lax.dynamic_slice_in_dim(query_unit, low_at, own_low, 1)
+    gain_own = lax.dynamic_slice_in_dim(gain_query, low_at, own_low, 0)
+    compact_gain = jnp.sum(compact_own * unit_own, 0)
+    latent_grad = (query_scale * (compact_own * gain_own - unit_own * mean_back)).astype(bf16)
+    kv_back = jnp.where(is_key, rotate(kv_back, kv_cos, -kv_sin), kv_back).astype(bf16)
+    kv_padded = lax.dynamic_update_slice_in_dim(
+        jnp.zeros((length, HEAD), bf16), kv_back, kv_at * kv_rows, 0
+    )
+    entry_sent = jnp.concatenate([latent_grad, kv_padded], -1)
+    entry_part = dot_transposed(entry_sent, entry_weights)
+    entry_grad = lax.psum_scatter(
+        entry_part.astype(bf16), "seq", scatter_dimension=0, tiled=True
+    ).astype(f32)
+    first_grad = jnp.sum(entry_part * (inputs_wide * entry_scale), 0)
+    own_at = seq_at * own_rows
+    inputs_own = layer_input[0].astype(f32)
+    scale_own = lax.dynamic_slice_in_dim(entry_scale, own_at, own_rows, 0)
+    entry_unit = inputs_own * scale_own
+    entry_scaled = entry_grad * gain_first
+    inputs_grad = scale_own * (
+        entry_scaled - entry_unit * jnp.mean(entry_scaled * entry_unit, -1, keepdims=True)
+    )
+    inputs_grad = inputs_grad + mid_grad
+
+    blocks = row_count * seq_count
+    weight_grad = dot_across(normed_in, entry_sent).astype(bf16)
+    weight_grad = weight_grad.reshape(blocks, down_rows, own_low + HEAD)
+    mine = (jnp.arange(seq_count) == seq_at)[None, :, None]
+    gain_back = jnp.where(mine, compact_gain.reshape(row_count, 1, low_part), 0.0)
+    extra = jnp.zeros((blocks, spare, own_low + HEAD), f32)
+    extra = extra.at[:, 0, :down_rows].set(first_grad.reshape(blocks, down_rows))
+    extra = extra.at[:, 1, :down_rows].set(second_grad.reshape(blocks, down_rows))
+    extra = extra.at[:, 2, :low_part].set(gain_back.reshape(blocks, low_part))
+    weight_grad = jnp.concatenate([weight_grad, extra.astype(bf16)], 1)
+    weight_grad = weight_grad.reshape(blocks * (down_rows + spare), own_low + HEAD)
+    weight_grad = lax.psum_scatter(weight_grad, "dp", scatter_dimension=0, tiled=True)
+    weight_grad = lax.all_to_all(weight_grad, "seq", 0, 0, tiled=True).astype(f32)
+    weight_grad = weight_grad.reshape(seq_count, down_rows + spare, own_low + HEAD)
+    compress_grad = weight_grad[:, :down_rows, :own_low].reshape(
+        seq_count, down_rows, row_count, low_part
+    )
+    compress_grad = compress_grad.transpose(1, 2, 0, 3).reshape(down_rows, low_width)
+    keymap_grad = jnp.sum(weight_grad[:kv_parts, :down_rows, own_low:], 0)
+    valuemap_grad = jnp.sum(weight_grad[kv_parts:, :down_rows, own_low:], 0)
+    gain_rows = jnp.sum(weight_grad[:, down_rows:], 0)
+    return (
+        layer_out[None],
+        inputs_grad[None],
+        gain_rows[0, :down_rows],
+        compress_grad,
+        gain_rows[2, :low_part],
+        lifted_grad.astype(f32),
+        keymap_grad,
+        valuemap_grad,
+        output_grad.astype(f32),
+        gain_rows[1, :down_rows],
+        feed_grads[0].astype(f32),
+        feed_grads[1].astype(f32),
+        feed_grads[2].astype(f32),
+    )
+
+
 def solution(mesh):
+    row_count, seq_count = mesh.shape["dp"], mesh.shape["seq"]
+    if row_count % 2 == 0 and seq_count % 2 == 0 and HEADS * 2 == row_count * seq_count:
+        local = functools.partial(local_heads, row_count, seq_count)
+    else:
+        local = local_tokens
     return jax.shard_map(
         local,
         mesh=mesh,

time: 2100 us -> 1030 us (0.49)
  waiting for transfers between devices: 1780 us -> 663 us
  other arithmetic: 25.9 us -> 99 us
  local copies, waits for them, and re-layouts: 32.5 us -> 85.7 us
  blocking collectives: 81.3 us -> 33.6 us
  matrix products: 163 us -> 119 us
    reduce_scatter x8 -> x7, waiting for transfers between devices: 1160 us -> 213 us  [the longest x1 49.1 us: local_heads(): lax.psum_scatter(matmul(hidden, w_down).astype(bf16), 'seq', scatter_dime...]
    all_gather x8, waiting for transfers between devices: 386 us -> 249 us  [the longest x1 45 us: local_heads(): inputs_all = lax.all_gather(layer_input[0], 'seq', axis=0, tiled=True)]
    unnamed x2 -> x0, blocking collectives: 81.3 us -> none
    psum x1, waiting for transfers between devices: 223 us -> 170 us  [local_heads(): feed_grads = lax.psum((gating_grad, upward_grad, down_grad), 'dp')]
    all_to_all x0 -> x2, blocking collectives: none -> 33.6 us  [the longest x1 19.8 us: local_heads(): sent = lax.all_to_all(sent, 'seq', 0, 0, tiled=True)]
    convert_element_type x9 -> x16, other arithmetic: 10.8 us -> 34.2 us  [the longest x1 5.27 us: local_heads(): feed_grads[0].astype(f32)]
    dot_general x8 -> x6, matrix products: 49 us -> 29.6 us  [dot_across(): lax.dot_general(left_op, right_op, (((0,), (0,)), ((), ())), preferred_el...]
    dot_general x8 -> x6, matrix products: 42.6 us -> 33.4 us  [dot_transposed(): lax.dot_general(left_op, right_op, (((1,), (1,)), ((), ())), preferred_el...]
  transfers between devices with their start and end apart: 17 -> 21, of which waited for: 17 -> 17; matrix products, arithmetic and copies ran while one was open for 7% -> 16% of each run, Pallas kernels for 0% -> 0%
where the time goes in v1:
time: 1030 us; the launch traced here: 1020 us
  waiting for transfers between devices  663 us (64%)
  matrix products  119 us (12%)
  other arithmetic  99 us (10%)
  local copies, waits for them, and re-layouts  85.7 us (8%)
  blocking collectives  33.6 us (3%)
  between operations  15 us (1%)
    psum x1, waiting for transfers between devices, local_heads(): feed_grads = lax.psum((gating_grad, upward_grad, down_grad), 'dp')  170 us
    reduce_scatter x1, waiting for transfers between devices, local_heads(): lax.psum_scatter(matmul(hidden, w_down).astype(bf16), 'seq', scatter_dime...  49.1 us
    reduce_scatter x1, waiting for transfers between devices, local_heads(): lax.psum_scatter(mixed, 'seq', scatter_dimension=0, tiled=True).astype(f32)  48.9 us
    reduce_scatter x1, waiting for transfers between devices, local_heads(): lax.psum_scatter(normed_grad.astype(bf16), 'seq', scatter_dimension=0, ti...  48.8 us
    all_gather x1, waiting for transfers between devices, local_heads(): inputs_all = lax.all_gather(layer_input[0], 'seq', axis=0, tiled=True)  45 us
    all_gather x1, waiting for transfers between devices, local_heads(): normed_all = lax.all_gather(normed_mid, 'seq', axis=0, tiled=True)  44.7 us
    reduce_scatter x1, waiting for transfers between devices, local_heads(): lax.psum_scatter(entry_part.astype(bf16), 'seq', scatter_dimension=0, til...  39.9 us
    all_gather x1, waiting for transfers between devices, local_heads(): attn_grad = lax.all_gather(mid_grad.astype(bf16), 'seq', axis=0, tiled=True)  35.3 us
  transfers between devices with their start and end apart: 21, of which 17 were waited for; matrix products, arithmetic and copies ran while one was open for 16% of the time, Pallas kernels for 0%

profile of v1, /device:TPU:0, one launch (start us, length us, event | category | flops | bytes accessed | tf_op | source)
XLA Modules:
  0.0 1024.3 jit_solution(1601993176118397460)
XLA Ops:
  18.1 19.8 %all_to_all.39 = bf16[8,72,384]{2,1,0:T(8,128)(2,1)} all-to-all(bf16[8,72,384]{2,1,0:T(8,128)(2,1)S(1)} %pad_maximum_fusion.8), channel_id=1, replica_groups=mesh['dp'=4,'seq'=8] {'seq'}, dimensions={0} | all-to-all | bytes 884736 | tf_op jit(solution)/shard_map/all_to_all | solution.py:335
  55.6 14.1 %all-gather.13.cloned.1.call-done = bf16[2304,384]{1,0:T(8,128)(2,1)} async-done(((bf16[576,384]{1,0:T(8,128)(2,1)}), bf16[2304,384]{1,0:T(8,128)(2,1)}) %all-gather.13.cloned.1.call-update) | async-done | bytes 1769488 | tf_op jit(solution)/shard_map/all_gather | solution.py:336
  73.4 45.0 %all-gather.21.cloned.1.call-done = bf16[1,1024,2048]{2,1,0:T(8,128)(2,1)} async-done(((bf16[1,128,2048]{2,1,0:T(8,128)(2,1)}), bf16[1,1024,2048]{2,1,0:T(8,128)(2,1)}) %all-gather.21.cloned.1.call-update) | async-done | bytes 4194320 | tf_op jit(solution)/shard_map/all_gather | solution.py:344
  128.1 26.3 %all-gather.25.cloned.1.call-done = bf16[512,2048]{1,0:T(8,128)(2,1)} async-done(((bf16[128,2048]{1,0:T(8,128)(2,1)}), bf16[512,2048]{1,0:T(8,128)(2,1)}) %all-gather.25.cloned.1.call-update) | async-done | bytes 2097168 | tf_op jit(solution)/shard_map/all_gather | solution.py:353
  164.2 18.5 %all-gather.15.cloned.1.call-done = bf16[1024,512]{1,0:T(8,128)(2,1)} async-done(((bf16[256,512]{1,0:T(8,128)(2,1)}), bf16[1024,512]{1,0:T(8,128)(2,1)}) %all-gather.15.cloned.1.call-update) | async-done | bytes 1048592 | tf_op jit(solution)/shard_map/all_gather | solution.py:349
  192.3 30.7 %all-gather.23.cloned.1.call-done = bf16[12288,128]{1,0:T(8,128)(2,1)} async-done(((bf16[1536,128]{1,0:T(8,128)(2,1)}), bf16[12288,128]{1,0:T(8,128)(2,1)}) %all-gather.23.cloned.1.call-update) | async-done | bytes 3145744 | tf_op jit(solution)/shard_map/all_gather | solution.py:381
  229.9 10.3 %fusion.139 = bf16[1024,8,128]{2,1,0:T(8,128)(2,1)} fusion(f32[8,128]{1,0:T(8,128)S(1)} %reshape.669, f32[1024]{0:T(1024)S(1)} %add_rsqrt_fusion, bf16[8,1024,128]{2,1,0:T(8,128)(2,1)S(1)} %slice.283), kind=kLoop, calls=%fused_computation.187 | loop fusion | flops 4194304 | bytes 4202496 | tf_op jit(solution)/shard_map/mul | solution.py:390
  251.8 8.0 fusion.94
  270.4 48.9 %reduce-scatter.11.cloned.1.call-done = bf16[128,2048]{1,0:T(8,128)(2,1)} async-done(((bf16[1024,2048]{1,0:T(8,128)(2,1)}), bf16[128,2048]{1,0:T(8,128)(2,1)}) %reduce-scatter.11.cloned.1.call-update) | async-done | bytes 524304 | tf_op jit(solution)/shard_map/reduce_scatter | solution.py:408
  323.5 44.7 %all-gather.17.cloned.1.call-done = bf16[1024,2048]{1,0:T(8,128)(2,1)} async-done(((bf16[128,2048]{1,0:T(8,128)(2,1)}), bf16[1024,2048]{1,0:T(8,128)(2,1)}) %all-gather.17.cloned.1.call-update) | async-done | bytes 4194320 | tf_op jit(solution)/shard_map/all_gather | solution.py:414
  368.1 8.0 fusion.97
  380.9 34.8 %all-gather.27.cloned.1.call-done = bf16[1,1024,2048]{2,1,0:T(8,128)(2,1)} async-done(((bf16[1,128,2048]{2,1,0:T(8,128)(2,1)}), bf16[1,1024,2048]{2,1,0:T(8,128)(2,1)}) %all-gather.27.cloned.1.call-update) | async-done | bytes 4194320 | tf_op jit(solution)/shard_map/all_gather | solution.py:364
  415.6 8.7 multiply_convert_fusion.2
  433.3 48.8 %reduce-scatter.15.cloned.1.call-done = bf16[128,2048]{1,0:T(8,128)(2,1)} async-done(((bf16[1024,2048]{1,0:T(8,128)(2,1)}), bf16[128,2048]{1,0:T(8,128)(2,1)}) %reduce-scatter.15.cloned.1.call-update) | async-done | bytes 524304 | tf_op jit(solution)/shard_map/reduce_scatter | solution.py:425
  496.6 35.3 %all-gather.19.cloned.1.call-done = bf16[1024,2048]{1,0:T(8,128)(2,1)} async-done(((bf16[128,2048]{1,0:T(8,128)(2,1)}), bf16[1024,2048]{1,0:T(8,128)(2,1)}) %all-gather.19.cloned.1.call-update) | async-done | bytes 4194320 | tf_op jit(solution)/shard_map/all_gather | solution.py:443
  564.6 6.6 multiply_reduce_fusion.1
  587.2 6.9 multiply_convert_fusion.1
  599.1 26.4 %reduce-scatter.17.cloned.1.call-done = bf16[1,1552,128]{2,1,0:T(8,128)(2,1)} async-done(((bf16[8,1552,128]{2,1,0:T(8,128)(2,1)}), bf16[1,1552,128]{2,1,0:T(8,128)(2,1)}) %reduce-scatter.17.cloned.1.call-update) | async-done | bytes 397328 | tf_op jit(solution)/shard_map/reduce_scatter | solution.py:477
  651.1 7.5 convolution_convert_fusion.3
  684.5 13.8 %all_to_all.40 = bf16[8,32,512]{2,1,0:T(8,128)(2,1)} all-to-all(bf16[8,32,512]{2,1,0:T(8,128)(2,1)} %bitcast.261), channel_id=1, replica_groups=mesh['dp'=4,'seq'=8] {'seq'}, dimensions={0} | all-to-all | bytes 524288 | tf_op jit(solution)/shard_map/all_to_all | solution.py:496
  702.5 170.5 %all-reduce.6.cloned.1.call-done = (bf16[2048,704]{0,1:T(8,128)(2,1)}, bf16[2048,704]{0,1:T(8,128)(2,1)}, bf16[704,2048]{1,0:T(8,128)(2,1)}) async-done(((bf16[2048,704]{0,1:T(8,128)(2,1)}, bf16[2048,704]{0,1:T(8,128)(2,1)}, bf16[704,2048]{1,0:T(8,128)(2,1)}), (bf16[2048,704]{0,1:T(8,128)(2,1)}, bf16[2048,704]{0,1:T(8,128)(2,1)}, bf16[704,2048]{1,0:T(8,128)(2,1)})) %all-reduce.6.cloned.1.call-update) | async-done | bytes 8650768 | tf_op jit(solution)/shard_map/psum | solution.py:431
  891.3 19.8 %reduce-scatter.25.cloned.1.call-done = bf16[1,128,2048]{2,1,0:T(8,128)(2,1)} async-done(((bf16[4,128,2048]{2,1,0:T(8,128)(2,1)}), bf16[1,128,2048]{2,1,0:T(8,128)(2,1)}) %reduce-scatter.25.cloned.1.call-update) | async-done | bytes 524304
  923.4 39.9 %reduce-scatter.19.cloned.1.call-done = bf16[128,2048]{1,0:T(8,128)(2,1)} async-done(((bf16[1024,2048]{1,0:T(8,128)(2,1)}), bf16[128,2048]{1,0:T(8,128)(2,1)}) %reduce-scatter.19.cloned.1.call-update) | async-done | bytes 524304 | tf_op jit(solution)/shard_map/reduce_scatter | solution.py:516
  964.7 49.1 %reduce-scatter.13.cloned.1.call-done = bf16[128,2048]{1,0:T(8,128)(2,1)} async-done(((bf16[1024,2048]{1,0:T(8,128)(2,1)}), bf16[128,2048]{1,0:T(8,128)(2,1)}) %reduce-scatter.13.cloned.1.call-update) | async-done | bytes 524304 | tf_op jit(solution)/shard_map/reduce_scatter | solution.py:432
  (285 shorter events, 267.1 us)
Async XLA Ops:
  7.2 408.5 %copy-start = (bf16[704,2048]{1,0:T(8,128)(2,1)S(1)}, bf16[704,2048]{1,0:T(8,128)(2,1)}, u32[]{:S(2)}) copy-start(bf16[704,2048]{1,0:T(8,128)(2,1)} %param.38) | copy-start | bytes 8650756
  7.2 62.4 %all-gather.13.cloned.1.call-start = ((), (), s32[]{:S(2)}) async-start(), calls=%async_computation.12 | async-start | bytes 2211840 | tf_op jit(solution)/shard_map/all_gather | solution.py:336
  38.0 80.4 %all-gather.21.cloned.1.call-start = ((), (), s32[]{:S(2)}) async-start(), calls=%async_computation.23 | async-start | bytes 4718592 | tf_op jit(solution)/shard_map/all_gather | solution.py:344
  38.7 115.6 %all-gather.25.cloned.1.call-start = ((), (), s32[]{:S(2)}) async-start(), calls=%async_computation.25 | async-start | bytes 2621440 | tf_op jit(solution)/shard_map/all_gather | solution.py:353
  41.7 13.8 %all-to-all-start.1 = ((bf16[8,32,512]{2,1,0:T(8,128)(2,1)}), bf16[8,32,512]{2,1,0:T(8,128)(2,1)}, u32[]{:S(2)}, u32[]{:S(2)}) async-start(bf16[8,32,512]{2,1,0:T(8,128)(2,1)} %all_to_all.28), calls=%async_computation.1 | async-start | bytes 524288 | tf_op jit(solution)/shard_map/all_to_all | solution.py:348
  45.7 136.9 %all-gather.15.cloned.1.call-start = ((), (), s32[]{:S(2)}) async-start(), calls=%async_computation.13 | async-start | bytes 1310720 | tf_op jit(solution)/shard_map/all_gather | solution.py:349
  55.5 167.5 %all-gather.23.cloned.1.call-start = ((), (), s32[]{:S(2)}) async-start(), calls=%async_computation.24 | async-start | bytes 3538944 | tf_op jit(solution)/shard_map/all_gather | solution.py:381
  127.8 191.5 %reduce-scatter.11.cloned.1.call-start = ((), (), s32[]{:S(2)}) async-start(), calls=%async_computation.14 | async-start | bytes 4718592 | tf_op jit(solution)/shard_map/reduce_scatter | solution.py:408
  157.4 30.8 %collective-permute-start = (bf16[2,128,2048]{2,1,0:T(8,128)(2,1)}, bf16[2,128,2048]{2,1,0:T(8,128)(2,1)}, u32[]{:S(2)}, u32[]{:S(2)}) collective-permute-start(bf16[2,128,2048]{2,1,0:T(8,128)(2,1)} %get-tuple-element.149), channel_id=1, source_target_pairs={{0,1},{1,0},{2,3},{3,2},{4,5},{5,4},{6,7},{7,6},{8,9},{9,8},{10,11... | collective-permute-start | bytes 3145736 | tf_op jit(solution)/shard_map/ppermute | solution.py:356
  270.3 97.9 %all-gather.17.cloned.1.call-start = ((), (), s32[]{:S(2)}) async-start(), calls=%async_computation.15 | async-start | bytes 4718592 | tf_op jit(solution)/shard_map/all_gather | solution.py:414
  320.6 163.3 %copy-start.31 = (f32[128]{0:T(128)}, f32[128]{0:T(128)S(1)}, u32[]{:S(2)}) copy-start(f32[128]{0:T(128)S(1)} %add_rsqrt_fusion.2) | copy-start | bytes 1540
  322.7 93.0 %all-gather.27.cloned.1.call-start = ((), (), s32[]{:S(2)}) async-start(), calls=%async_computation.26 | async-start | bytes 4718592 | tf_op jit(solution)/shard_map/all_gather | solution.py:364
  323.4 158.7 %reduce-scatter.15.cloned.1.call-start = ((), (), s32[]{:S(2)}) async-start(), calls=%async_computation.17 | async-start | bytes 4718592 | tf_op jit(solution)/shard_map/reduce_scatter | solution.py:425
  433.3 98.7 %all-gather.19.cloned.1.call-start = ((), (), s32[]{:S(2)}) async-start(), calls=%async_computation.18 | async-start | bytes 4718592 | tf_op jit(solution)/shard_map/all_gather | solution.py:443
  486.5 139.0 %reduce-scatter.17.cloned.1.call-start = ((), (), s32[]{:S(2)}) async-start(), calls=%async_computation.19 | async-start | bytes 3575808 | tf_op jit(solution)/shard_map/reduce_scatter | solution.py:477
  585.9 98.6 %reduce-scatter.23.cloned.1.call-start = ((), (), s32[]{:S(2)}) async-start(), calls=%async_computation.22 | async-start | bytes 1310720 | tf_op jit(solution)/shard_map/reduce_scatter | solution.py:495
  599.1 99.2 %reduce-scatter.21.cloned.1.call-start = ((), (), s32[]{:S(2)}) async-start(), calls=%async_computation.21 | async-start | bytes 2211840 | tf_op jit(solution)/shard_map/reduce_scatter | solution.py:541
  651.0 222.0 %all-reduce.6.cloned.1.call-start = ((), (), s32[]{:S(2)}) async-start(), calls=%async_computation.28 | async-start | bytes 17301504 | tf_op jit(solution)/shard_map/psum | solution.py:431
  667.8 243.3 %reduce-scatter.25.cloned.1.call-start = ((), (), s32[]{:S(2)}) async-start(), calls=%async_computation.27 | async-start | bytes 2621440
  672.9 2.7 collective-permute-start.1
  677.3 286.0 %reduce-scatter.19.cloned.1.call-start = ((), (), s32[]{:S(2)}) async-start(), calls=%async_computation.20 | async-start | bytes 4718592 | tf_op jit(solution)/shard_map/reduce_scatter | solution.py:516
  677.9 335.9 %reduce-scatter.13.cloned.1.call-start = ((), (), s32[]{:S(2)}) async-start(), calls=%async_computation.16 | async-start | bytes 4718592 | tf_op jit(solution)/shard_map/reduce_scatter | solution.py:432
  698.3 214.9 %all-to-all-start.2 = ((bf16[8,72,384]{2,1,0:T(8,128)(2,1)}), bf16[8,72,384]{2,1,0:T(8,128)(2,1)}, u32[]{:S(2)}, u32[]{:S(2)}) async-start(bf16[8,72,384]{2,1,0:T(8,128)(2,1)} %bitcast.260), calls=%async_computation.8 | async-start | bytes 884736 | tf_op jit(solution)/shard_map/all_to_all | solution.py:542
  914.8 99.0 %copy-start.37 = (f32[128]{0:T(128)S(1)}, f32[128]{0:T(128)}, u32[]{:S(2)}) copy-start(f32[128]{0:T(128)} %copy-done.36) | copy-start | bytes 1540
  (47 other events, 401.9 us)
Sparse Core Ops, SparseCore 0:
  38.1 31.4 all-gather.12
  71.2 47.1 all-gather.20
  120.3 34.0 all-gather.24
  156.0 26.6 all-gather.14
  184.7 38.2 all-gather.22
  270.4 48.8 reduce-scatter.10
  322.8 45.3 all-gather.16
  369.7 45.8 all-gather.26
  433.4 48.7 reduce-scatter.14
  486.6 45.2 all-gather.18
  586.0 39.3 reduce-scatter.16
  628.8 26.5 reduce-scatter.22
  658.7 32.4 reduce-scatter.20
  696.1 176.8 all-reduce.5
  875.8 35.1 reduce-scatter.24
  913.3 49.9 reduce-scatter.18
  965.6 48.1 reduce-scatter.12

commit v2 on v1

--- a/solution.py
+++ b/solution.py
@@ -3,6 +3,8 @@
 import jax
 import jax.numpy as jnp
 from jax import lax
+from jax.experimental import pallas as pl
+from jax.experimental.pallas import tpu as pltpu
 from jax.sharding import PartitionSpec as P
 
 HEADS = 16
@@ -277,6 +279,336 @@
         feed_grads[0],
         feed_grads[1],
         feed_grads[2],
+    )
+
+
+def tie(*values):
+    return lax.optimization_barrier(values)
+
+
+def gather_rows(block, row_count):
+    row_at = lax.axis_index("dp")
+    result = jnp.zeros((row_count,) + block.shape, block.dtype)
+    result = lax.dynamic_update_index_in_dim(result, block, row_at, 0)
+    for hop in range(1, row_count):
+        moved = lax.ppermute(block, "dp", [(i, i ^ hop) for i in range(row_count)])
+        result = lax.dynamic_update_index_in_dim(result, moved, row_at ^ hop, 0)
+    return result
+
+
+def sum_rows(blocks, row_count):
+    row_at = lax.axis_index("dp")
+    total = lax.dynamic_index_in_dim(blocks, row_at, 0, False).astype(jnp.float32)
+    for hop in range(1, row_count):
+        given = lax.dynamic_index_in_dim(blocks, row_at ^ hop, 0, False)
+        moved = lax.ppermute(given, "dp", [(i, i ^ hop) for i in range(row_count)])
+        total = total + moved.astype(jnp.float32)
+    return total
+
+
+def swap_rows(block, hop):
+    return lax.ppermute(block, "dp", [(i, i ^ hop) for i in range(4)])
+
+
+class SquareSum:
+    def __init__(self, product, size, axis, first, second):
+        row_at = lax.axis_index("dp")
+        self.product, self.axis = product, axis
+        self.first, self.second = first, second
+        self.half, self.quarter = size // 2, size // 4
+        self.upper_half = (row_at // first) % 2
+        self.upper_quarter = (row_at // second) % 2
+
+    def make(self, half, quarter):
+        return self.product(half * self.half + quarter * self.quarter, self.quarter)
+
+    def give(self, quarter):
+        return self.make(1 - self.upper_half, quarter).astype(jnp.bfloat16)
+
+    def give_passed(self):
+        return self.give(1 - self.upper_quarter)
+
+    def give_kept(self):
+        return self.give(self.upper_quarter)
+
+    def send(self, block):
+        return swap_rows(block, self.first)
+
+    def pass_on(self, moved):
+        own = self.make(self.upper_half, 1 - self.upper_quarter)
+        return swap_rows((own + moved.astype(jnp.float32)).astype(jnp.bfloat16), self.second)
+
+    def finish(self, moved, passed):
+        own = self.make(self.upper_half, self.upper_quarter)
+        return (own + moved.astype(jnp.float32) + passed.astype(jnp.float32)).astype(
+            jnp.bfloat16
+        )
+
+    def spread_once(self, own):
+        return swap_rows(own, self.first), swap_rows(own, self.second)
+
+    def spread_twice(self, beside):
+        return swap_rows(beside, self.first)
+
+    def assemble(self, result, base, own, across, beside, far):
+        for block, half, quarter in (
+            (own, self.upper_half, self.upper_quarter),
+            (beside, self.upper_half, 1 - self.upper_quarter),
+            (across, 1 - self.upper_half, self.upper_quarter),
+            (far, 1 - self.upper_half, 1 - self.upper_quarter),
+        ):
+            start = base + half * self.half + quarter * self.quarter
+            result = lax.dynamic_update_slice_in_dim(
+                result, block.astype(jnp.float32), start, self.axis
+            )
+        return result
+
+
+def turn(block, cosine, sine):
+    half = block.shape[-1] // 2
+    first, second = block[:, :half], block[:, half:]
+    return jnp.concatenate([first * cosine - second * sine, second * cosine + first * sine], -1)
+
+
+def kv_block(kv_ref, at):
+    rows = kv_ref.shape[1] // 2
+    return jnp.concatenate([kv_ref[at, :rows], kv_ref[at, rows:]], -1)
+
+
+def low_block(low_ref, gain_ref):
+    low = jnp.concatenate([low_ref[i] for i in range(low_ref.shape[0])], -1).astype(jnp.float32)
+    gain = jnp.concatenate([gain_ref[i : i + 1] for i in range(gain_ref.shape[0])], -1)
+    scale = lax.rsqrt(jnp.mean(low * low, -1, keepdims=True) + epsilon)
+    return low * scale, gain
+
+
+def block_weights(query, kv_ref, seg_query_ref, seg_key_ref, step, parts):
+    rows = query.shape[0]
+    keys = jnp.concatenate([kv_block(kv_ref, j) for j in range(step + 1)], 0)
+    logits = dot_transposed(query, keys) * query.shape[1] ** (-0.5)
+    count = (step + 1) * rows
+    row_at = step * rows + lax.broadcasted_iota(jnp.int32, (rows, count), 0)
+    col_at = lax.broadcasted_iota(jnp.int32, (rows, count), 1)
+    allowed = (col_at <= row_at) & (seg_query_ref[...] == seg_key_ref[:, :count])
+    logits = jnp.where(allowed, logits, masked_value)
+    powers = jnp.exp(logits - jnp.max(logits, -1, keepdims=True))
+    return powers / jnp.sum(powers, -1, keepdims=True), keys
+
+
+def attend_kernel(
+    parts,
+    low_ref,
+    kv_ref,
+    gain_ref,
+    cosine_ref,
+    sine_ref,
+    seg_query_ref,
+    seg_key_ref,
+    up_ref,
+    out_ref,
+    mixed_ref,
+    queries_ref,
+    attended_ref,
+    norm_ref,
+):
+    def block(step):
+        unit, gain = low_block(low_ref, gain_ref)
+        query_norm = (unit * gain).astype(jnp.bfloat16)
+        norm_ref[...] = query_norm
+        raw = matmul(query_norm, up_ref[...])
+        values = jnp.concatenate([kv_block(kv_ref, parts + j) for j in range(step + 1)], 0)
+        for head in range(raw.shape[1] // HEAD):
+            cols = slice(head * HEAD, (head + 1) * HEAD)
+            query = turn(raw[:, cols], cosine_ref[...], sine_ref[...]).astype(jnp.bfloat16)
+            queries_ref[:, cols] = query
+            weights, _ = block_weights(query, kv_ref, seg_query_ref, seg_key_ref, step, parts)
+            attended_ref[:, cols] = matmul(weights.astype(jnp.bfloat16), values).astype(
+                jnp.bfloat16
+            )
+        mixed_ref[...] = matmul(attended_ref[...], out_ref[...]).astype(jnp.bfloat16)
+
+    for step in range(parts):
+        pl.when(pl.program_id(0) == step)(functools.partial(block, step))
+
+
+def attend_back_kernel(
+    parts,
+    grad_ref,
+    queries_ref,
+    low_ref,
+    kv_ref,
+    gain_ref,
+    cosine_ref,
+    sine_ref,
+    seg_query_ref,
+    seg_key_ref,
+    up_ref,
+    out_ref,
+    back_ref,
+    query_grad_ref,
+    keys_sum,
+    values_sum,
+    means,
+):
+    slots = low_ref.shape[0]
+    lanes = low_ref.shape[2]
+
+    def block(step):
+        unit, gain = low_block(low_ref, gain_ref)
+        rows = unit.shape[0]
+        scale_value = HEAD ** (-0.5)
+        context = dot_transposed(grad_ref[...], out_ref[...]).astype(jnp.bfloat16)
+        values = jnp.concatenate([kv_block(kv_ref, parts + j) for j in range(step + 1)], 0)
+        count = (step + 1) * rows
+        last = slice(step * rows, count)
+        keys_sum[last] = jnp.zeros((rows, HEAD), jnp.float32)
+        values_sum[last] = jnp.zeros((rows, HEAD), jnp.float32)
+        for head in range(context.shape[1] // HEAD):
+            cols = slice(head * HEAD, (head + 1) * HEAD)
+            query = queries_ref[:, cols]
+            weights, keys = block_weights(query, kv_ref, seg_query_ref, seg_key_ref, step, parts)
+            probs = dot_transposed(context[:, cols], values)
+            inner = jnp.sum(weights * probs, -1, keepdims=True)
+            logit_grad = (weights * (probs - inner)).astype(jnp.bfloat16)
+            turned = matmul(logit_grad, keys) * scale_value
+            query_grad_ref[:, cols] = turn(turned, cosine_ref[...], -sine_ref[...]).astype(
+                jnp.bfloat16
+            )
+            keys_sum[:count] += dot_across(logit_grad, query) * scale_value
+            values_sum[:count] += dot_across(weights.astype(jnp.bfloat16), context[:, cols])
+        compact = dot_transposed(query_grad_ref[...], up_ref[...])
+        for slot in range(slots):
+            back_ref[slot, last] = compact[:, slot * lanes : (slot + 1) * lanes].astype(
+                jnp.bfloat16
+            )
+        mean = jnp.sum(compact * gain * unit, -1, keepdims=True) / compact.shape[1]
+        mean = jnp.broadcast_to(mean, (rows, lanes)).T
+        for part in range(rows // lanes):
+            at = step * (rows // lanes) + part
+            means[at : at + 1] = mean[:1, part * lanes : (part + 1) * lanes]
+        if step == parts - 1:
+            length = parts * rows
+            mean_high = means[...].astype(jnp.bfloat16)
+            mean_low = (means[...] - mean_high.astype(jnp.float32)).astype(jnp.bfloat16)
+            tail = length + 2 * rows
+            size = means.shape[0]
+            for slot in range(slots):
+                total = keys_sum if slot < parts else values_sum
+                own = total[(slot % parts) * rows : (slot % parts + 1) * rows].astype(jnp.bfloat16)
+                back_ref[slot, length : length + rows] = own[:, :lanes]
+                back_ref[slot, length + rows : tail] = own[:, lanes:]
+                back_ref[slot, tail : tail + size] = mean_high
+                back_ref[slot, tail + size : tail + 2 * size] = mean_low
+
+    for step in range(parts):
+        pl.when(pl.program_id(0) == step)(functools.partial(block, step))
+
+
+def attention_specs(parts, slots, length, lanes, low_width, head_width, width):
+    rows = length // parts
+    return [
+        pl.BlockSpec((slots, rows, lanes), lambda i: (0, i, 0)),
+        pl.BlockSpec((slots, 2 * rows, lanes), lambda i: (0, length // (2 * rows), 0)),
+        pl.BlockSpec((slots, lanes), lambda i: (0, 0)),
+        pl.BlockSpec((rows, HEAD // 2), lambda i: (i, 0)),
+        pl.BlockSpec((rows, HEAD // 2), lambda i: (i, 0)),
+        pl.BlockSpec((rows, 1), lambda i: (i, 0)),
+        pl.BlockSpec((1, length), lambda i: (0, 0)),
+        pl.BlockSpec((low_width, head_width), lambda i: (0, 0)),
+        pl.BlockSpec((head_width, width), lambda i: (0, 0)),
+    ]
+
+
+def attend(parts, low_all, gain, cosine, sine, segment_row, up_mine, out_mine):
+    slots, _, lanes = low_all.shape
+    length = segment_row.shape[0]
+    low_width, head_width = up_mine.shape
+    width = out_mine.shape[1]
+    rows = length // parts
+    bf16 = jnp.bfloat16
+    return pl.pallas_call(
+        functools.partial(attend_kernel, parts),
+        grid=(parts,),
+        in_specs=attention_specs(parts, slots, length, lanes, low_width, head_width, width),
+        out_specs=[
+            pl.BlockSpec((rows, width), lambda i: (i, 0)),
+            pl.BlockSpec((rows, head_width), lambda i: (i, 0)),
+            pl.BlockSpec((rows, head_width), lambda i: (i, 0)),
+            pl.BlockSpec((rows, low_width), lambda i: (i, 0)),
+        ],
+        out_shape=[
+            jax.ShapeDtypeStruct((length, width), bf16),
+            jax.ShapeDtypeStruct((length, head_width), bf16),
+            jax.ShapeDtypeStruct((length, head_width), bf16),
+            jax.ShapeDtypeStruct((length, low_width), bf16),
+        ],
+        compiler_params=pltpu.CompilerParams(vmem_limit_bytes=48 * 1024 * 1024),
+        cost_estimate=pl.CostEstimate(
+            flops=8 * 10**9, bytes_accessed=16 * 10**6, transcendentals=2 * 10**6
+        ),
+        name="attend",
+    )(
+        low_all,
+        low_all,
+        gain,
+        cosine,
+        sine,
+        segment_row[:, None],
+        segment_row[None],
+        up_mine,
+        out_mine,
+    )
+
+
+def attend_back(
+    parts, grad, queries, low_all, gain, cosine, sine, segment_row, up_mine, out_mine
+):
+    slots, _, lanes = low_all.shape
+    length = segment_row.shape[0]
+    low_width, head_width = up_mine.shape
+    width = out_mine.shape[1]
+    rows = length // parts
+    means = length // lanes
+    total = length + 2 * rows + 2 * means
+    bf16 = jnp.bfloat16
+    return pl.pallas_call(
+        functools.partial(attend_back_kernel, parts),
+        grid=(parts,),
+        in_specs=[
+            pl.BlockSpec((rows, width), lambda i: (i, 0)),
+            pl.BlockSpec((rows, head_width), lambda i: (i, 0)),
+        ]
+        + attention_specs(parts, slots, length, lanes, low_width, head_width, width),
+        out_specs=[
+            pl.BlockSpec((slots, total, lanes), lambda i: (0, 0, 0)),
+            pl.BlockSpec((rows, head_width), lambda i: (i, 0)),
+        ],
+        out_shape=[
+            jax.ShapeDtypeStruct((slots, total, lanes), bf16),
+            jax.ShapeDtypeStruct((length, head_width), bf16),
+        ],
+        scratch_shapes=[
+            pltpu.VMEM((length, HEAD), jnp.float32),
+            pltpu.VMEM((length, HEAD), jnp.float32),
+            pltpu.VMEM((means, lanes), jnp.float32),
+        ],
+        compiler_params=pltpu.CompilerParams(vmem_limit_bytes=48 * 1024 * 1024),
+        cost_estimate=pl.CostEstimate(
+            flops=12 * 10**9, bytes_accessed=20 * 10**6, transcendentals=2 * 10**6
+        ),
+        name="attend_back",
+    )(
+        grad,
+        queries,
+        low_all,
+        low_all,
+        gain,
+        cosine,
+        sine,
+        segment_row[:, None],
+        segment_row[None],
+        up_mine,
+        out_mine,
     )
 
 
@@ -333,7 +665,7 @@
     )
     sent = sent.reshape(seq_count * (down_rows + spare), own_low + HEAD)
     sent = lax.all_to_all(sent, "seq", 0, 0, tiled=True)
-    entry_all = lax.all_gather(sent, "dp", axis=0, tiled=True)
+    entry_all = gather_rows(sent, row_count)
     entry_all = entry_all.reshape(row_count * seq_count, down_rows + spare, own_low + HEAD)
     entry_weights = entry_all[:, :down_rows].reshape(width, own_low + HEAD)
     gain_first = entry_all[:, down_rows, :down_rows].reshape(width).astype(f32)
@@ -346,11 +678,11 @@
     up_sent = query_up.reshape(up_rows, 2, half_count, chips, HEAD).transpose(3, 1, 0, 2, 4)
     up_sent = up_sent.reshape(seq_count * up_rows, own_heads * HEAD)
     up_mine = lax.all_to_all(up_sent, "seq", 0, 0, tiled=True)
-    up_mine = lax.all_gather(up_mine, "dp", axis=0, tiled=True)
+    up_mine = gather_rows(up_mine, row_count)
     up_mine = up_mine.reshape(row_count, seq_count, low_part, own_heads * HEAD)
     up_mine = up_mine.transpose(1, 0, 2, 3).reshape(low_width, own_heads * HEAD)
 
-    out_all = lax.all_gather(out_proj, "dp", axis=0, tiled=False)
+    out_all = gather_rows(out_proj, row_count)
     out_kept = lax.dynamic_slice_in_dim(out_all, core_at * half_count, half_count, 0)
     out_given = lax.dynamic_slice_in_dim(out_all, (1 - core_at) * half_count, half_count, 0)
     out_got = lax.ppermute(out_given, "seq", swap)
@@ -379,40 +711,22 @@
         [low_own[:, :own_low].astype(bf16), kv_own[:, :half_head], kv_own[:, half_head:]], 0
     )
     low_all = lax.all_gather(low_sent, "seq", axis=0, tiled=False)
-    query_low = low_all[:, :length].transpose(1, 0, 2).reshape(length, low_width).astype(f32)
-    kv_all = jnp.concatenate(
-        [low_all[:, length : length + kv_rows], low_all[:, length + kv_rows :]], -1
-    )
-    key_all = kv_all[:kv_parts].reshape(length, HEAD)
-    value_all = kv_all[kv_parts:].reshape(length, HEAD)
-
-    query_scale = lax.rsqrt(jnp.mean(query_low * query_low, -1, keepdims=True) + epsilon)
-    query_norm = (query_low * query_scale * gain_query).astype(bf16)
-    query_raw = matmul(query_norm, up_mine).reshape(length, own_heads, HEAD)
-    queries = rotate(query_raw, cosine_table[:, None, :], sine_table[:, None, :]).astype(bf16)
-    queries = queries.transpose(1, 0, 2)
+
     segment_row = segment_ids[0]
-    allowed = (positions[None, :] <= positions[:, None]) & (
-        segment_row[None, :] == segment_row[:, None]
-    )
-    scale_value = HEAD ** (-0.5)
-    logits = (
-        jnp.einsum("htd,sd->hts", queries, key_all, preferred_element_type=f32) * scale_value
-    )
-    masked = jnp.where(allowed[None], logits, masked_value)
-    attention = jax.nn.softmax(masked, axis=-1)
-    attention_low = attention.astype(bf16)
-    attended = jnp.einsum("hts,sd->htd", attention_low, value_all, preferred_element_type=f32)
-    attended = attended.astype(bf16).transpose(1, 0, 2).reshape(length, own_heads * HEAD)
-    mixed = matmul(attended, out_mine).astype(bf16)
+    gain_slots = gain_query.reshape(seq_count, own_low)
+    half_cos, half_sin = cosine_table[:, :half_head], sine_table[:, :half_head]
+    mixed, queries, attended, query_norm = attend(
+        kv_parts, low_all, gain_slots, half_cos, half_sin, segment_row, up_mine, out_mine
+    )
     mixed = lax.psum_scatter(mixed, "seq", scatter_dimension=0, tiled=True).astype(f32)
     mid_sum = layer_input[0].astype(f32) + mixed
     mid_scale = lax.rsqrt(jnp.mean(mid_sum * mid_sum, -1, keepdims=True) + epsilon)
     mid_unit = mid_sum * mid_scale
     normed_mid = (mid_unit * gain_second).astype(bf16)
 
+    grad_hidden = dot_transposed(cot_all, w_down)
+    normed_mid, grad_hidden = tie(normed_mid, grad_hidden)
     normed_all = lax.all_gather(normed_mid, "seq", axis=0, tiled=True)
-    grad_hidden = dot_transposed(cot_all, w_down)
     gate_pre = matmul(normed_all, w_gate)
     up_pre = matmul(normed_all, w_up)
     hidden = gated_unit(gate_pre, up_pre)
@@ -425,14 +739,32 @@
     normed_grad = lax.psum_scatter(
         normed_grad.astype(bf16), "seq", scatter_dimension=0, tiled=True
     ).astype(f32)
-    down_grad = dot_across(hidden, cot_all).astype(bf16)
-    gating_grad = dot_across(normed_all, gate_grad).astype(bf16)
-    upward_grad = dot_across(normed_all, up_grad).astype(bf16)
-    feed_grads = lax.psum((gating_grad, upward_grad, down_grad), "dp")
-    branch_out = lax.psum_scatter(
-        matmul(hidden, w_down).astype(bf16), "seq", scatter_dimension=0, tiled=True
-    )
-    layer_out = mid_sum + branch_out.astype(f32)
+    def from_columns(left, right):
+        return lambda start, size: dot_across(
+            lax.dynamic_slice_in_dim(left, start, size, 1), right
+        )
+
+    def to_columns(left, right, base):
+        return lambda start, size: dot_across(
+            left, lax.dynamic_slice_in_dim(right, base + start, size, 1)
+        )
+
+    half_width = width // 2
+    sums = [
+        SquareSum(from_columns(normed_all, gate_grad), width, 0, 1, 2),
+        SquareSum(from_columns(normed_all, up_grad), width, 0, 2, 1),
+        SquareSum(to_columns(hidden, cot_all, 0), half_width, 1, 1, 2),
+        SquareSum(to_columns(hidden, cot_all, half_width), half_width, 1, 2, 1),
+    ]
+    passed = [one.send(one.give_passed()) for one in sums]
+    kept = [one.give_kept() for one in sums]
+    hidden_out = matmul(hidden, w_down).astype(bf16)
+    moved = [one.send(block) for one, block in zip(sums[2:], kept[2:])]
+    normed_grad, kept[0], kept[1], hidden_out, moved, passed = tie(
+        normed_grad, kept[0], kept[1], hidden_out, moved, passed
+    )
+    moved = [one.send(block) for one, block in zip(sums[:2], kept[:2])] + moved
+    passed = [one.pass_on(block) for one, block in zip(sums, passed)]
 
     second_grad = jnp.sum(normed_grad * mid_unit, 0)
     scaled_grad = normed_grad * gain_second
@@ -442,40 +774,20 @@
     mid_grad = mid_grad + cot_rows.astype(f32)
     attn_grad = lax.all_gather(mid_grad.astype(bf16), "seq", axis=0, tiled=True)
 
-    context_grad = dot_transposed(attn_grad, out_mine).astype(bf16)
-    context_grad = context_grad.reshape(length, own_heads, HEAD).transpose(1, 0, 2)
-    probs_grad = jnp.einsum("htd,sd->hts", context_grad, value_all, preferred_element_type=f32)
-    inner_sum = jnp.sum(attention * probs_grad, -1, keepdims=True)
-    logit_grad = (attention * (probs_grad - inner_sum)).astype(bf16)
-    queries_grad = (
-        jnp.einsum("hts,sd->htd", logit_grad, key_all, preferred_element_type=f32) * scale_value
-    )
-    keys_grad = (
-        jnp.einsum("hts,htd->sd", logit_grad, queries, preferred_element_type=f32) * scale_value
-    )
-    values_grad = jnp.einsum(
-        "hts,htd->sd", attention_low, context_grad, preferred_element_type=f32
-    )
-    query_grad = rotate(queries_grad, cosine_table, -sine_table).astype(bf16)
-    query_grad = query_grad.transpose(1, 0, 2).reshape(length, own_heads * HEAD)
-    compact_grad = dot_transposed(query_grad, up_mine)
-    query_unit = query_low * query_scale
-    compact_mean = jnp.sum(compact_grad * gain_query * query_unit, -1) / low_width
-    mean_rows = compact_mean.reshape(length // own_low, own_low)
-    compact_sent = compact_grad.astype(bf16).reshape(length, seq_count, own_low).transpose(1, 0, 2)
-    kv_sent = jnp.concatenate([keys_grad, values_grad], 0).astype(bf16)
-    kv_sent = kv_sent.reshape(seq_count, kv_rows, HEAD)
-    mean_high = mean_rows.astype(bf16)
-    mean_low = (mean_rows - mean_high.astype(f32)).astype(bf16)
-    means = jnp.broadcast_to(
-        jnp.concatenate([mean_high, mean_low], 0)[None],
-        (seq_count, 2 * mean_rows.shape[0], own_low),
-    )
-    back_sent = jnp.concatenate(
-        [compact_sent, kv_sent[:, :, :half_head], kv_sent[:, :, half_head:], means], 1
-    )
-    back = lax.psum_scatter(back_sent, "seq", scatter_dimension=0, tiled=False).astype(f32)
-
+    attn_grad, moved, passed, hidden_out = tie(attn_grad, moved, passed, hidden_out)
+    branch_out = lax.psum_scatter(hidden_out, "seq", scatter_dimension=0, tiled=True)
+    back_sent, query_grad = attend_back(
+        kv_parts,
+        attn_grad,
+        queries,
+        low_all,
+        gain_slots,
+        half_cos,
+        half_sin,
+        segment_row,
+        up_mine,
+        out_mine,
+    )
     output_grad = dot_across(attended, attn_grad).astype(bf16)
     output_grad = output_grad.reshape(own_heads, 2, out_rows, width)
     grad_kept = lax.dynamic_index_in_dim(output_grad, core_at, 1, False)
@@ -486,16 +798,17 @@
         jnp.concatenate([grad_kept, grad_got], 0),
         jnp.concatenate([grad_got, grad_kept], 0),
     )
-    output_grad = lax.psum_scatter(output_grad, "dp", scatter_dimension=0, tiled=False)
+    output_grad = sum_rows(output_grad, row_count)
+    owned = [one.finish(block, more) for one, block, more in zip(sums, moved, passed)]
+    spread = [one.spread_once(block) for one, block in zip(sums[2:], owned[2:])]
+    back_sent, branch_out, output_grad, owned[0], owned[1], spread = tie(
+        back_sent, branch_out, output_grad, owned[0], owned[1], spread
+    )
+    spread = [one.spread_once(block) for one, block in zip(sums[:2], owned[:2])] + spread
+    back = lax.psum_scatter(back_sent, "seq", scatter_dimension=0, tiled=False).astype(f32)
 
     lifted_grad = dot_across(query_norm, query_grad).astype(bf16)
-    lifted_grad = lifted_grad.reshape(seq_count, row_count, up_rows, own_heads * HEAD)
-    lifted_grad = lifted_grad.transpose(1, 0, 2, 3)
-    lifted_grad = lifted_grad.reshape(row_count * seq_count * up_rows, own_heads * HEAD)
-    lifted_grad = lax.psum_scatter(lifted_grad, "dp", scatter_dimension=0, tiled=True)
-    lifted_grad = lax.all_to_all(lifted_grad, "seq", 0, 0, tiled=True)
-    lifted_grad = lifted_grad.reshape(chips, 2, up_rows, half_count, HEAD)
-    lifted_grad = lifted_grad.transpose(2, 1, 3, 0, 4).reshape(up_rows, HEADS * HEAD)
+    back, lifted_grad, spread = tie(back, lifted_grad, spread)
 
     compact_own = back[:length]
     kv_back = jnp.concatenate(
@@ -503,7 +816,11 @@
     )
     mean_back = back[length + 2 * kv_rows :].reshape(2, length).sum(0)[:, None]
     low_at = seq_at * own_low
-    unit_own = lax.dynamic_slice_in_dim(query_unit, low_at, own_low, 1)
+    query_low = low_all[:, :length].astype(f32)
+    query_scale = jnp.sum(query_low * query_low, (0, 2)) / low_width
+    query_scale = lax.rsqrt(query_scale + epsilon)[:, None]
+    low_mine = lax.dynamic_index_in_dim(low_all, seq_at, 0, False)[:length].astype(f32)
+    unit_own = low_mine * query_scale
     gain_own = lax.dynamic_slice_in_dim(gain_query, low_at, own_low, 0)
     compact_gain = jnp.sum(compact_own * unit_own, 0)
     latent_grad = (query_scale * (compact_own * gain_own - unit_own * mean_back)).astype(bf16)
@@ -513,20 +830,23 @@
     )
     entry_sent = jnp.concatenate([latent_grad, kv_padded], -1)
     entry_part = dot_transposed(entry_sent, entry_weights)
+    blocks_of = [
+        (own, across, beside, one.spread_twice(beside))
+        for one, own, (across, beside) in zip(sums, owned, spread)
+    ]
+    units = w_gate.shape[1]
+    gating_grad = sums[0].assemble(jnp.zeros((width, units), f32), 0, *blocks_of[0])
+    upward_grad = sums[1].assemble(jnp.zeros((width, units), f32), 0, *blocks_of[1])
+    down_grad = sums[2].assemble(jnp.zeros((units, width), f32), 0, *blocks_of[2])
+    down_grad = sums[3].assemble(down_grad, half_width, *blocks_of[3])
+    lifted_grad = lifted_grad.reshape(seq_count, row_count, up_rows, own_heads * HEAD)
+    lifted_grad = lifted_grad.transpose(1, 0, 2, 3)
+    lifted_grad = lifted_grad.reshape(row_count, seq_count * up_rows, own_heads * HEAD)
+    lifted_grad = sum_rows(lifted_grad, row_count).astype(bf16)
     entry_grad = lax.psum_scatter(
         entry_part.astype(bf16), "seq", scatter_dimension=0, tiled=True
     ).astype(f32)
     first_grad = jnp.sum(entry_part * (inputs_wide * entry_scale), 0)
-    own_at = seq_at * own_rows
-    inputs_own = layer_input[0].astype(f32)
-    scale_own = lax.dynamic_slice_in_dim(entry_scale, own_at, own_rows, 0)
-    entry_unit = inputs_own * scale_own
-    entry_scaled = entry_grad * gain_first
-    inputs_grad = scale_own * (
-        entry_scaled - entry_unit * jnp.mean(entry_scaled * entry_unit, -1, keepdims=True)
-    )
-    inputs_grad = inputs_grad + mid_grad
-
     blocks = row_count * seq_count
     weight_grad = dot_across(normed_in, entry_sent).astype(bf16)
     weight_grad = weight_grad.reshape(blocks, down_rows, own_low + HEAD)
@@ -537,8 +857,10 @@
     extra = extra.at[:, 1, :down_rows].set(second_grad.reshape(blocks, down_rows))
     extra = extra.at[:, 2, :low_part].set(gain_back.reshape(blocks, low_part))
     weight_grad = jnp.concatenate([weight_grad, extra.astype(bf16)], 1)
-    weight_grad = weight_grad.reshape(blocks * (down_rows + spare), own_low + HEAD)
-    weight_grad = lax.psum_scatter(weight_grad, "dp", scatter_dimension=0, tiled=True)
+    weight_grad = weight_grad.reshape(
+        row_count, seq_count * (down_rows + spare), own_low + HEAD
+    )
+    weight_grad = sum_rows(weight_grad, row_count).astype(bf16)
     weight_grad = lax.all_to_all(weight_grad, "seq", 0, 0, tiled=True).astype(f32)
     weight_grad = weight_grad.reshape(seq_count, down_rows + spare, own_low + HEAD)
     compress_grad = weight_grad[:, :down_rows, :own_low].reshape(
@@ -548,6 +870,24 @@
     keymap_grad = jnp.sum(weight_grad[:kv_parts, :down_rows, own_low:], 0)
     valuemap_grad = jnp.sum(weight_grad[kv_parts:, :down_rows, own_low:], 0)
     gain_rows = jnp.sum(weight_grad[:, down_rows:], 0)
+    lifted_grad = lax.all_to_all(lifted_grad, "seq", 0, 0, tiled=True)
+    lifted_grad = lifted_grad.reshape(chips, 2, up_rows, half_count, HEAD)
+    lifted_grad = lifted_grad.transpose(2, 1, 3, 0, 4).reshape(up_rows, HEADS * HEAD)
+
+    entry_grad, compress_grad, lifted_grad, output_grad, spread = tie(
+        entry_grad, compress_grad, lifted_grad, output_grad, spread
+    )
+    layer_out = mid_sum + branch_out.astype(f32)
+    own_at = seq_at * own_rows
+    inputs_own = layer_input[0].astype(f32)
+    scale_own = lax.dynamic_slice_in_dim(entry_scale, own_at, own_rows, 0)
+    entry_unit = inputs_own * scale_own
+    entry_scaled = entry_grad * gain_first
+    inputs_grad = scale_own * (
+        entry_scaled - entry_unit * jnp.mean(entry_scaled * entry_unit, -1, keepdims=True)
+    )
+    inputs_grad = inputs_grad + mid_grad
+
     return (
         layer_out[None],
         inputs_grad[None],
@@ -559,15 +899,15 @@
         valuemap_grad,
         output_grad.astype(f32),
         gain_rows[1, :down_rows],
-        feed_grads[0].astype(f32),
-        feed_grads[1].astype(f32),
-        feed_grads[2].astype(f32),
+        gating_grad,
+        upward_grad,
+        down_grad,
     )
 
 
 def solution(mesh):
     row_count, seq_count = mesh.shape["dp"], mesh.shape["seq"]
-    if row_count % 2 == 0 and seq_count % 2 == 0 and HEADS * 2 == row_count * seq_count:
+    if row_count == 4 and seq_count % 2 == 0 and HEADS * 2 == row_count * seq_count:
         local = functools.partial(local_heads, row_count, seq_count)
     else:
         local = local_tokens

time: 1030 us -> 624 us (0.61)
  waiting for transfers between devices: 663 us -> 279 us
  starting transfers between devices: 9.16 us -> 68.3 us
  blocking collectives: 33.6 us -> 0 us
  matrix products: 119 us -> 86.5 us
  Pallas kernels: 0 us -> 27.8 us
  local copies, waits for them, and re-layouts: 85.7 us -> 62.2 us
  other arithmetic: 99 us -> 76.5 us
    psum x1 -> x0, waiting for transfers between devices: 170 us -> none  [local_heads(): feed_grads = lax.psum((gating_grad, upward_grad, down_grad), 'dp')]
    ppermute x0 -> x42, waiting for transfers between devices: none -> 79.9 us  [the longest x24 40 us: swap_rows(): return lax.ppermute(block, 'dp', [(i, i ^ hop) for i in range(4)])]
    all_gather x3 -> x0, waiting for transfers between devices: 58.8 us -> none  [the longest x1 26.3 us: local_heads(): out_all = lax.all_gather(out_proj, 'dp', axis=0, tiled=False)]
    reduce_scatter x3 -> x1, waiting for transfers between devices: 49.1 us -> 0.01 us  [local_heads(): lax.psum_scatter(hidden_out, 'seq', scatter_dimension=0, tiled=True)]
    ppermute x0 -> x42, starting transfers between devices: none -> 47.6 us  [the longest x24 26.4 us: swap_rows(): return lax.ppermute(block, 'dp', [(i, i ^ hop) for i in range(4)])]
    all_gather x1, waiting for transfers between devices: 45 us -> 0.01 us  [local_heads(): inputs_all = lax.all_gather(layer_input[0], 'seq', axis=0, tiled=True)]
    reduce_scatter x1, waiting for transfers between devices: 39.9 us -> 0.01 us  [local_heads(): lax.psum_scatter(entry_part.astype(bf16), 'seq', scatter_dimension=0, til...]
    reduce_scatter x1, waiting for transfers between devices: 48.8 us -> 11.1 us  [local_heads(): lax.psum_scatter(normed_grad.astype(bf16), 'seq', scatter_dimension=0, ti...]
  transfers between devices with their start and end apart: 21 -> 58, of which waited for: 17 -> 22; matrix products, arithmetic and copies ran while one was open for 16% -> 26% of each run, Pallas kernels for 0% -> 5%
where the time goes in v2:
time: 624 us; the launch traced here: 616 us
  waiting for transfers between devices  279 us (45%)
  matrix products  86.5 us (14%)
  other arithmetic  76.5 us (12%)
  starting transfers between devices  68.3 us (11%)
  local copies, waits for them, and re-layouts  62.2 us (10%)
  Pallas kernels  27.8 us (4%)
  between operations  15.7 us (3%)
    all_gather x1, waiting for transfers between devices, local_heads(): normed_all = lax.all_gather(normed_mid, 'seq', axis=0, tiled=True)  45.4 us
    reduce_scatter x1, waiting for transfers between devices, local_heads(): lax.psum_scatter(mixed, 'seq', scatter_dimension=0, tiled=True).astype(f32)  43.6 us
    dot_general x19, matrix products, dot_across(): lax.dot_general(left_op, right_op, (((0,), (0,)), ((), ())), preferred_el...  43.5 us
    ppermute x24, waiting for transfers between devices, swap_rows(): return lax.ppermute(block, 'dp', [(i, i ^ hop) for i in range(4)])  40 us
    reduce_scatter x1, waiting for transfers between devices, local_heads(): lax.psum_scatter(back_sent, 'seq', scatter_dimension=0, tiled=False)  30.8 us
    dynamic_update_slice x16, other arithmetic, assemble(): lax.dynamic_update_slice_in_dim(result, block.astype(jnp.float32), start,...  29.4 us
    ppermute x9, waiting for transfers between devices, sum_rows(): moved = lax.ppermute(given, 'dp', [(i, i ^ hop) for i in range(row_count)])  26.6 us
    ppermute x24, starting transfers between devices, swap_rows(): return lax.ppermute(block, 'dp', [(i, i ^ hop) for i in range(4)])  26.4 us
  transfers between devices with their start and end apart: 58, of which 22 were waited for; matrix products, arithmetic and copies ran while one was open for 26% of the time, Pallas kernels for 5%

profile of v2, /device:TPU:0, one launch (start us, length us, event | category | flops | bytes accessed | tf_op | source)
XLA Modules:
  0.0 615.5 jit_solution(15942047756072737837)
XLA Ops:
  18.5 6.3 %all-to-all-start = ((bf16[8,72,384]{2,1,0:T(8,128)(2,1)}), bf16[8,72,384]{2,1,0:T(8,128)(2,1)S(1)}, u32[]{:S(2)}, u32[]{:S(2)}) async-start(bf16[8,72,384]{2,1,0:T(8,128)(2,1)} %pad_maximum_fusion.5), calls=%async_computation | async-start | bytes 884736 | tf_op jit(solution)/shard_map/all_to_all | solution.py:667
  24.9 25.8 %all-to-all-done = bf16[8,72,384]{2,1,0:T(8,128)(2,1)S(1)} async-done(((bf16[8,72,384]{2,1,0:T(8,128)(2,1)}), bf16[8,72,384]{2,1,0:T(8,128)(2,1)S(1)}, u32[]{:S(2)}, u32[]{:S(2)}) %all-to-all-start) | async-done | bytes 442400 | tf_op jit(solution)/shard_map/all_to_all | solution.py:667
  59.1 4.7 collective-permute-done
  64.9 8.3 %collective-permute-done.1 = bf16[576,384]{1,0:T(8,128)(2,1)} collective-permute-done((bf16[576,384]{1,0:T(8,128)(2,1)S(1)}, bf16[576,384]{1,0:T(8,128)(2,1)}, u32[]{:S(2)}, u32[]{:S(2)}) %collective-permute-start.1) | collective-permute-done | bytes 442400 | tf_op jit(solution)/shard_map/ppermute | solution.py:294
  103.1 9.5 %all-to-all-done.1 = bf16[8,32,512]{2,1,0:T(8,128)(2,1)} async-done(((bf16[8,32,512]{2,1,0:T(8,128)(2,1)}), bf16[8,32,512]{2,1,0:T(8,128)(2,1)}, u32[]{:S(2)}, u32[]{:S(2)}) %all-to-all-start.1) | async-done | bytes 262176 | tf_op jit(solution)/shard_map/all_to_all | solution.py:680
  135.7 12.1 %attend.1 = (bf16[1024,2048]{1,0:T(8,128)(2,1)}, bf16[1024,512]{1,0:T(8,128)(2,1)S(1)}, bf16[1024,512]{1,0:T(8,128)(2,1)S(1)}, bf16[1024,1024]{1,0:T(8,128)(2,1)}) custom-call(bf16[8,1536,128]{2,1,0:T(8,128)(2,1)} %bitcast.237, bf16[8,1536,128]{2,1,0:T(8,128)(2,1)} %bitcast.238, f32[8,128]{1,0:T(8,128)S(1)} %reshape.450.gain_ref, ...), custom_call_target="tpu_custom_call" | custom-call | flops 8000000000 | bytes 16000000 | tf_op jit(solution)/shard_map/attend/pallas_call | solution.py:529
  150.3 25.3 %all-gather.17.cloned.1.call-done = bf16[1,1024,2048]{2,1,0:T(8,128)(2,1)} async-done(((bf16[1,128,2048]{2,1,0:T(8,128)(2,1)}), bf16[1,1024,2048]{2,1,0:T(8,128)(2,1)}) %all-gather.17.cloned.1.call-update) | async-done | bytes 4194320 | tf_op jit(solution)/shard_map/all_gather | solution.py:696
  175.6 7.8 %fusion.5 = f32[1024,704]{0,1:T(8,128)} fusion(bf16[704,2048]{1,0:T(8,128)(2,1)} %param.38, bf16[1,1024,2048]{2,1,0:T(8,128)(2,1)} %all-gather.17.cloned.1.call-done), kind=kOutput, calls=%fused_computation.9 | convolution fusion | flops 2952790016 | bytes 9961472 | tf_op jit(solution)/shard_map/dot_general | solution.py:47
  183.4 43.6 %reduce-scatter.6.cloned.1.call-done = bf16[128,2048]{1,0:T(8,128)(2,1)} async-done(((bf16[1024,2048]{1,0:T(8,128)(2,1)}), bf16[128,2048]{1,0:T(8,128)(2,1)}) %reduce-scatter.6.cloned.1.call-update) | async-done | bytes 524304 | tf_op jit(solution)/shard_map/reduce_scatter | solution.py:721
  230.8 45.4 %all-gather.9.cloned.1.call-done = bf16[1024,2048]{1,0:T(8,128)(2,1)} async-done(((bf16[128,2048]{1,0:T(8,128)(2,1)}), bf16[1024,2048]{1,0:T(8,128)(2,1)}) %all-gather.9.cloned.1.call-update) | async-done | bytes 4194320 | tf_op jit(solution)/shard_map/all_gather | solution.py:729
  276.2 6.0 fusion.101
  282.3 5.4 multiply_convert_fusion
  291.3 5.2 add_convert_fusion
  312.4 5.0 convolution_convert_fusion
  334.2 11.1 %reduce-scatter.8.cloned.1.call-done = bf16[128,2048]{1,0:T(8,128)(2,1)} async-done(((bf16[1024,2048]{1,0:T(8,128)(2,1)}), bf16[128,2048]{1,0:T(8,128)(2,1)}) %reduce-scatter.8.cloned.1.call-update) | async-done | bytes 524304 | tf_op jit(solution)/shard_map/reduce_scatter | solution.py:739
  368.5 30.6 %collective-permute-done.20 = bf16[704,256]{1,0:T(8,128)(2,1)S(1)} collective-permute-done((bf16[704,256]{1,0:T(8,128)(2,1)S(1)}, bf16[704,256]{1,0:T(8,128)(2,1)S(1)}, u32[]{:S(2)}, u32[]{:S(2)}) %collective-permute-start.20) | collective-permute-done | bytes 360480 | tf_op jit(solution)/shard_map/ppermute | solution.py:310
  414.2 15.7 %attend_back.1 = (bf16[8,1552,128]{2,1,0:T(8,128)(2,1)}, bf16[1024,512]{1,0:T(8,128)(2,1)S(1)}) custom-call(bf16[1024,2048]{1,0:T(8,128)(2,1)} %all-gather.11.cloned.1.call-done.grad_ref, bf16[1024,512]{1,0:T(8,128)(2,1)S(1)} %copy-done.12, bf16[8,1536,128]{2,1,0:T(8,128)(2,1)} %bitcast.239, bf16[8,1536,128]{2,1,0:T(8,128)(2,1)} %bitcast.240, ...), custom_call_target="tpu_custom_call" | custom-call | flops 12000000000 | bytes 20000000 | tf_op jit(solution)/shard_map/attend_back/pallas_call | solution.py:574
  445.9 8.8 %collective-permute-done.24 = bf16[128,2048]{1,0:T(8,128)(2,1)S(1)} collective-permute-done((bf16[128,2048]{1,0:T(8,128)(2,1)S(1)}, bf16[128,2048]{1,0:T(8,128)(2,1)S(1)}, u32[]{:S(2)}, u32[]{:S(2)}) %collective-permute-start.24) | collective-permute-done | bytes 524320 | tf_op jit(solution)/shard_map/ppermute | solution.py:304
  473.0 30.8 %reduce-scatter.12.cloned.1.call-done = bf16[1,1552,128]{2,1,0:T(8,128)(2,1)} async-done(((bf16[8,1552,128]{2,1,0:T(8,128)(2,1)}), bf16[1,1552,128]{2,1,0:T(8,128)(2,1)}) %reduce-scatter.12.cloned.1.call-update) | async-done | bytes 397328 | tf_op jit(solution)/shard_map/reduce_scatter | solution.py:808
  507.5 6.3 %fusion.3 = (bf16[2048]{0:T(1024)(128)(2,1)S(1)}, bf16[1024,2048]{1,0:T(8,128)(2,1)}) fusion(bf16[1,1024,2048]{2,1,0:T(8,128)(2,1)} %all-gather.13.cloned.1.call-done, f32[1024]{0:T(1024)S(1)} %add_rsqrt_fusion.1, bf16[2048,384]{1,0:T(8,128)(2,1)} %bitcast.245, bf16[1024,256]{1,0:T(8,128)(2,1)S(1)} %fusion.77, bf16[1024,128]{1,0:T(8,128)(2,1)S(1)} %get-tuple-element.227), kind=kOutput, calls=%fused_computation.5 | convolution fusion | flops 1622669312 | bytes 10756096 | tf_op jit(solution)/shard_map/dot_general | solution.py:47
  546.9 5.3 collective-permute-done.38
  568.4 7.0 %collective-permute-done.35 = bf16[576,384]{1,0:T(8,128)(2,1)} collective-permute-done((bf16[576,384]{1,0:T(8,128)(2,1)}, bf16[576,384]{1,0:T(8,128)(2,1)}, u32[]{:S(2)}, u32[]{:S(2)}) %collective-permute-start.35) | collective-permute-done | bytes 442400 | tf_op jit(solution)/shard_map/ppermute | solution.py:304
  577.5 5.1 all-to-all-start.2
  590.6 5.6 all-to-all-done.2
  (391 shorter events, 263.1 us)
Async XLA Ops:
  7.2 69.1 %all-gather.13.cloned.1.call-start = ((), (), s32[]{:S(2)}) async-start(), calls=%async_computation.16 | async-start | bytes 4718592 | tf_op jit(solution)/shard_map/all_gather | solution.py:676
  24.8 107.6 %all-gather.15.cloned.1.call-start = ((), (), s32[]{:S(2)}) async-start(), calls=%async_computation.17 | async-start | bytes 3538944 | tf_op jit(solution)/shard_map/all_gather | solution.py:713
  85.6 89.9 %all-gather.17.cloned.1.call-start = ((), (), s32[]{:S(2)}) async-start(), calls=%async_computation.18 | async-start | bytes 4718592 | tf_op jit(solution)/shard_map/all_gather | solution.py:696
  95.4 131.7 %reduce-scatter.6.cloned.1.call-start = ((), (), s32[]{:S(2)}) async-start(), calls=%async_computation.9 | async-start | bytes 4718592 | tf_op jit(solution)/shard_map/reduce_scatter | solution.py:721
  149.8 126.4 %all-gather.9.cloned.1.call-start = ((), (), s32[]{:S(2)}) async-start(), calls=%async_computation.10 | async-start | bytes 4718592 | tf_op jit(solution)/shard_map/all_gather | solution.py:729
  230.8 114.6 %reduce-scatter.8.cloned.1.call-start = ((), (), s32[]{:S(2)}) async-start(), calls=%async_computation.11 | async-start | bytes 4718592 | tf_op jit(solution)/shard_map/reduce_scatter | solution.py:739
  296.5 102.7 %all-gather.11.cloned.1.call-start = ((), (), s32[]{:S(2)}) async-start(), calls=%async_computation.12 | async-start | bytes 4718592 | tf_op jit(solution)/shard_map/all_gather | solution.py:775
  300.8 45.8 %collective-permute-start.13 = (bf16[512,704]{0,1:T(8,128)(2,1)}, bf16[512,704]{0,1:T(8,128)(2,1)}, u32[]{:S(2)}, u32[]{:S(2)}) collective-permute-start(bf16[512,704]{0,1:T(8,128)(2,1)} %convolution_convert_fusion.4), channel_id=1, source_target_pairs={{0,16},{8,24},{16,0},{24,8},{1,17},{9,25},{17,1},{25,9},{2,18},{10... | collective-permute-start | bytes 2162696 | tf_op jit(solution)/shard_map/ppermute | solution.py:310
  305.3 41.3 %collective-permute-start.12 = (bf16[512,704]{0,1:T(8,128)(2,1)}, bf16[512,704]{0,1:T(8,128)(2,1)}, u32[]{:S(2)}, u32[]{:S(2)}) collective-permute-start(bf16[512,704]{0,1:T(8,128)(2,1)} %convolution_convert_fusion.5), channel_id=1, source_target_pairs={{0,8},{8,0},{16,24},{24,16},{1,9},{9,1},{17,25},{25,17},{2,10},{10... | collective-permute-start | bytes 2162696 | tf_op jit(solution)/shard_map/ppermute | solution.py:310
  348.8 113.9 %reduce-scatter.10.cloned.1.call-start = ((), (), s32[]{:S(2)}) async-start(), calls=%async_computation.13 | async-start | bytes 4718592 | tf_op jit(solution)/shard_map/reduce_scatter | solution.py:778
  358.5 40.6 %collective-permute-start.19 = (bf16[512,704]{0,1:T(8,128)(2,1)S(1)}, bf16[512,704]{0,1:T(8,128)(2,1)S(1)}, u32[]{:S(2)}, u32[]{:S(2)}) collective-permute-start(bf16[512,704]{0,1:T(8,128)(2,1)S(1)} %add_convert_fusion.3), channel_id=1, source_target_pairs={{0,8},{8,0},{16,24},{24,16},{1,9},{9,1},{17,25},{25,17},{2,10},{10... | collective-permute-start | bytes 2162696 | tf_op jit(solution)/shard_map/ppermute | solution.py:310
  360.6 38.5 %collective-permute-start.18 = (bf16[512,704]{0,1:T(8,128)(2,1)S(1)}, bf16[512,704]{0,1:T(8,128)(2,1)}, u32[]{:S(2)}, u32[]{:S(2)}) collective-permute-start(bf16[512,704]{0,1:T(8,128)(2,1)S(1)} %add_convert_fusion.4), channel_id=1, source_target_pairs={{0,16},{8,24},{16,0},{24,8},{1,17},{9,25},{17,1},{25,9},{2,18},{10... | collective-permute-start | bytes 2162696 | tf_op jit(solution)/shard_map/ppermute | solution.py:310
  362.1 37.0 %collective-permute-start.16 = (bf16[512,704]{0,1:T(8,128)(2,1)S(1)}, bf16[512,704]{0,1:T(8,128)(2,1)}, u32[]{:S(2)}, u32[]{:S(2)}) collective-permute-start(bf16[512,704]{0,1:T(8,128)(2,1)S(1)} %copy-done.50), channel_id=1, source_target_pairs={{0,8},{8,0},{16,24},{24,16},{1,9},{9,1},{17,25},{25,17},{2,10},{10... | collective-permute-start | bytes 2162696 | tf_op jit(solution)/shard_map/ppermute | solution.py:310
  399.2 104.6 %reduce-scatter.12.cloned.1.call-start = ((), (), s32[]{:S(2)}) async-start(), calls=%async_computation.14 | async-start | bytes 3575808 | tf_op jit(solution)/shard_map/reduce_scatter | solution.py:808
  406.8 51.0 %collective-permute-start.28 = (bf16[704,256]{1,0:T(8,128)(2,1)S(1)}, bf16[704,256]{1,0:T(8,128)(2,1)S(1)}, u32[]{:S(2)}, u32[]{:S(2)}) collective-permute-start(bf16[704,256]{1,0:T(8,128)(2,1)S(1)} %add_convert_fusion.5), channel_id=1, source_target_pairs={{0,16},{8,24},{16,0},{24,8},{1,17},{9,25},{17,1},{25,9},{2,18},{10... | collective-permute-start | bytes 1081352 | tf_op jit(solution)/shard_map/ppermute | solution.py:310
  408.5 49.3 %collective-permute-start.29 = (bf16[704,256]{1,0:T(8,128)(2,1)S(1)}, bf16[704,256]{1,0:T(8,128)(2,1)}, u32[]{:S(2)}, u32[]{:S(2)}) collective-permute-start(bf16[704,256]{1,0:T(8,128)(2,1)S(1)} %add_convert_fusion.5), channel_id=1, source_target_pairs={{0,8},{8,0},{16,24},{24,16},{1,9},{9,1},{17,25},{25,17},{2,10},{10... | collective-permute-start | bytes 1081352 | tf_op jit(solution)/shard_map/ppermute | solution.py:310
  462.7 136.3 %reduce-scatter.14.cloned.1.call-start = ((), (), s32[]{:S(2)}) async-start(), calls=%async_computation.15 | async-start | bytes 4718592 | tf_op jit(solution)/shard_map/reduce_scatter | solution.py:846
  465.0 39.8 %collective-permute-start.30 = (bf16[512,704]{0,1:T(8,128)(2,1)S(1)}, bf16[512,704]{0,1:T(8,128)(2,1)}, u32[]{:S(2)}, u32[]{:S(2)}) collective-permute-start(bf16[512,704]{0,1:T(8,128)(2,1)S(1)} %get-tuple-element.166), channel_id=1, source_target_pairs={{0,8},{8,0},{16,24},{24,16},{1,9},{9,1},{17,25},{25,17},{2,10},{10... | collective-permute-start | bytes 2162696 | tf_op jit(solution)/shard_map/ppermute | solution.py:310
  466.4 38.5 %collective-permute-start.31 = (bf16[512,704]{0,1:T(8,128)(2,1)S(1)}, bf16[512,704]{0,1:T(8,128)(2,1)}, u32[]{:S(2)}, u32[]{:S(2)}) collective-permute-start(bf16[512,704]{0,1:T(8,128)(2,1)S(1)} %get-tuple-element.166), channel_id=1, source_target_pairs={{0,16},{8,24},{16,0},{24,8},{1,17},{9,25},{17,1},{25,9},{2,18},{10... | collective-permute-start | bytes 2162696 | tf_op jit(solution)/shard_map/ppermute | solution.py:310
  467.0 37.9 %collective-permute-start.32 = (bf16[512,704]{0,1:T(8,128)(2,1)S(1)}, bf16[512,704]{0,1:T(8,128)(2,1)}, u32[]{:S(2)}, u32[]{:S(2)}) collective-permute-start(bf16[512,704]{0,1:T(8,128)(2,1)S(1)} %get-tuple-element.167), channel_id=1, source_target_pairs={{0,16},{8,24},{16,0},{24,8},{1,17},{9,25},{17,1},{25,9},{2,18},{10... | collective-permute-start | bytes 2162696 | tf_op jit(solution)/shard_map/ppermute | solution.py:310
  468.4 36.5 %collective-permute-start.33 = (bf16[512,704]{0,1:T(8,128)(2,1)S(1)}, bf16[512,704]{0,1:T(8,128)(2,1)}, u32[]{:S(2)}, u32[]{:S(2)}) collective-permute-start(bf16[512,704]{0,1:T(8,128)(2,1)S(1)} %get-tuple-element.167), channel_id=1, source_target_pairs={{0,8},{8,0},{16,24},{24,16},{1,9},{9,1},{17,25},{25,17},{2,10},{10... | collective-permute-start | bytes 2162696 | tf_op jit(solution)/shard_map/ppermute | solution.py:310
  520.7 39.2 %collective-permute-start.42 = (bf16[704,256]{1,0:T(8,128)(2,1)}, bf16[704,256]{1,0:T(8,128)(2,1)}, u32[]{:S(2)}, u32[]{:S(2)}) collective-permute-start(bf16[704,256]{1,0:T(8,128)(2,1)} %collective-permute-done.27), channel_id=1, source_target_pairs={{0,8},{8,0},{16,24},{24,16},{1,9},{9,1},{17,25},{25,17},{2,10},{10... | collective-permute-start | bytes 1081352 | tf_op jit(solution)/shard_map/ppermute | solution.py:310
  522.2 62.9 %collective-permute-start.41 = (bf16[512,704]{0,1:T(8,128)(2,1)}, bf16[512,704]{0,1:T(8,128)(2,1)}, u32[]{:S(2)}, u32[]{:S(2)}) collective-permute-start(bf16[512,704]{0,1:T(8,128)(2,1)} %collective-permute-done.33), channel_id=1, source_target_pairs={{0,16},{8,24},{16,0},{24,8},{1,17},{9,25},{17,1},{25,9},{2,18},{10... | collective-permute-start | bytes 2162696 | tf_op jit(solution)/shard_map/ppermute | solution.py:310
  546.4 36.2 %collective-permute-start.43 = (bf16[704,256]{1,0:T(8,128)(2,1)}, bf16[704,256]{1,0:T(8,128)(2,1)}, u32[]{:S(2)}, u32[]{:S(2)}) collective-permute-start(bf16[704,256]{1,0:T(8,128)(2,1)} %collective-permute-done.29), channel_id=1, source_target_pairs={{0,16},{8,24},{16,0},{24,8},{1,17},{9,25},{17,1},{25,9},{2,18},{10... | collective-permute-start | bytes 1081352 | tf_op jit(solution)/shard_map/ppermute | solution.py:310
  (93 other events, 1288.3 us)
Sparse Core Ops, SparseCore 0:
  9.6 59.2 all-gather.12
  85.8 42.1 all-gather.14
  129.6 45.9 all-gather.16
  178.3 48.7 reduce-scatter.5
  230.9 45.2 all-gather.8
  296.6 48.7 reduce-scatter.7
  349.0 45.2 all-gather.10
  399.3 50.3 reduce-scatter.9
  462.9 40.9 reduce-scatter.11
  513.9 48.9 reduce-scatter.13

commit v3 on v2

--- a/solution.py
+++ b/solution.py
@@ -757,14 +757,11 @@
         SquareSum(to_columns(hidden, cot_all, half_width), half_width, 1, 2, 1),
     ]
     passed = [one.send(one.give_passed()) for one in sums]
-    kept = [one.give_kept() for one in sums]
+    moved = [one.send(one.give_kept()) for one in sums]
     hidden_out = matmul(hidden, w_down).astype(bf16)
-    moved = [one.send(block) for one, block in zip(sums[2:], kept[2:])]
-    normed_grad, kept[0], kept[1], hidden_out, moved, passed = tie(
-        normed_grad, kept[0], kept[1], hidden_out, moved, passed
-    )
-    moved = [one.send(block) for one, block in zip(sums[:2], kept[:2])] + moved
+    normed_grad, hidden_out, moved, passed = tie(normed_grad, hidden_out, moved, passed)
     passed = [one.pass_on(block) for one, block in zip(sums, passed)]
+    owned = [one.finish(block, more) for one, block, more in zip(sums, moved, passed)]
 
     second_grad = jnp.sum(normed_grad * mid_unit, 0)
     scaled_grad = normed_grad * gain_second
@@ -774,7 +771,7 @@
     mid_grad = mid_grad + cot_rows.astype(f32)
     attn_grad = lax.all_gather(mid_grad.astype(bf16), "seq", axis=0, tiled=True)
 
-    attn_grad, moved, passed, hidden_out = tie(attn_grad, moved, passed, hidden_out)
+    attn_grad, owned, hidden_out = tie(attn_grad, owned, hidden_out)
     branch_out = lax.psum_scatter(hidden_out, "seq", scatter_dimension=0, tiled=True)
     back_sent, query_grad = attend_back(
         kv_parts,
@@ -799,7 +796,6 @@
         jnp.concatenate([grad_got, grad_kept], 0),
     )
     output_grad = sum_rows(output_grad, row_count)
-    owned = [one.finish(block, more) for one, block, more in zip(sums, moved, passed)]
     spread = [one.spread_once(block) for one, block in zip(sums[2:], owned[2:])]
     back_sent, branch_out, output_grad, owned[0], owned[1], spread = tie(
         back_sent, branch_out, output_grad, owned[0], owned[1], spread
@@ -808,6 +804,10 @@
     back = lax.psum_scatter(back_sent, "seq", scatter_dimension=0, tiled=False).astype(f32)
 
     lifted_grad = dot_across(query_norm, query_grad).astype(bf16)
+    lifted_grad = lifted_grad.reshape(seq_count, row_count, up_rows, own_heads * HEAD)
+    lifted_grad = lifted_grad.transpose(1, 0, 2, 3)
+    lifted_grad = lifted_grad.reshape(row_count, seq_count * up_rows, own_heads * HEAD)
+    lifted_grad = sum_rows(lifted_grad, row_count).astype(bf16)
     back, lifted_grad, spread = tie(back, lifted_grad, spread)
 
     compact_own = back[:length]
@@ -839,10 +839,6 @@
     upward_grad = sums[1].assemble(jnp.zeros((width, units), f32), 0, *blocks_of[1])
     down_grad = sums[2].assemble(jnp.zeros((units, width), f32), 0, *blocks_of[2])
     down_grad = sums[3].assemble(down_grad, half_width, *blocks_of[3])
-    lifted_grad = lifted_grad.reshape(seq_count, row_count, up_rows, own_heads * HEAD)
-    lifted_grad = lifted_grad.transpose(1, 0, 2, 3)
-    lifted_grad = lifted_grad.reshape(row_count, seq_count * up_rows, own_heads * HEAD)
-    lifted_grad = sum_rows(lifted_grad, row_count).astype(bf16)
     entry_grad = lax.psum_scatter(
         entry_part.astype(bf16), "seq", scatter_dimension=0, tiled=True
     ).astype(f32)
@@ -860,7 +856,11 @@
     weight_grad = weight_grad.reshape(
         row_count, seq_count * (down_rows + spare), own_low + HEAD
     )
+    lifted_grad = lax.all_to_all(lifted_grad, "seq", 0, 0, tiled=True)
+    lifted_grad = lifted_grad.reshape(chips, 2, up_rows, half_count, HEAD)
+    lifted_grad = lifted_grad.transpose(2, 1, 3, 0, 4).reshape(up_rows, HEADS * HEAD)
     weight_grad = sum_rows(weight_grad, row_count).astype(bf16)
+    weight_grad, lifted_grad = tie(weight_grad, lifted_grad)
     weight_grad = lax.all_to_all(weight_grad, "seq", 0, 0, tiled=True).astype(f32)
     weight_grad = weight_grad.reshape(seq_count, down_rows + spare, own_low + HEAD)
     compress_grad = weight_grad[:, :down_rows, :own_low].reshape(
@@ -870,10 +870,6 @@
     keymap_grad = jnp.sum(weight_grad[:kv_parts, :down_rows, own_low:], 0)
     valuemap_grad = jnp.sum(weight_grad[kv_parts:, :down_rows, own_low:], 0)
     gain_rows = jnp.sum(weight_grad[:, down_rows:], 0)
-    lifted_grad = lax.all_to_all(lifted_grad, "seq", 0, 0, tiled=True)
-    lifted_grad = lifted_grad.reshape(chips, 2, up_rows, half_count, HEAD)
-    lifted_grad = lifted_grad.transpose(2, 1, 3, 0, 4).reshape(up_rows, HEADS * HEAD)
-
     entry_grad, compress_grad, lifted_grad, output_grad, spread = tie(
         entry_grad, compress_grad, lifted_grad, output_grad, spread
     )

time: 624 us -> 615 us (0.986)
  matrix products: 86.5 us -> 78.2 us
    ppermute x24, waiting for transfers between devices: 40 us -> 53.4 us  [swap_rows(): return lax.ppermute(block, 'dp', [(i, i ^ hop) for i in range(4)])]
    reduce_scatter x1, waiting for transfers between devices: 30.8 us -> 21.2 us  [local_heads(): lax.psum_scatter(back_sent, 'seq', scatter_dimension=0, tiled=False)]
    dot_general x19, matrix products: 43.5 us -> 35.3 us  [dot_across(): lax.dot_general(left_op, right_op, (((0,), (0,)), ((), ())), preferred_el...]
    reduce_scatter x1, waiting for transfers between devices: 11.1 us -> 3.23 us  [local_heads(): lax.psum_scatter(normed_grad.astype(bf16), 'seq', scatter_dimension=0, ti...]
    dynamic_update_slice x16 -> x15, other arithmetic: 29.4 us -> 24.8 us  [assemble(): lax.dynamic_update_slice_in_dim(result, block.astype(jnp.float32), start,...]
    unnamed x127 -> x121, local copies, waits for them, and re-layouts: 20.5 us -> 23.5 us
  transfers between devices with their start and end apart: 58 -> 58, of which waited for: 22 -> 28; matrix products, arithmetic and copies ran while one was open for 26% -> 23% of each run, Pallas kernels for 5% -> 5%
where the time goes in v3:
time: 615 us; the launch traced here: 606 us
  waiting for transfers between devices  280 us (46%)
  matrix products  78.2 us (13%)
  other arithmetic  73.1 us (12%)
  starting transfers between devices  72.9 us (12%)
  local copies, waits for them, and re-layouts  59 us (10%)
  Pallas kernels  27.8 us (5%)
  between operations  15.9 us (3%)
    ppermute x24, waiting for transfers between devices, swap_rows(): return lax.ppermute(block, 'dp', [(i, i ^ hop) for i in range(4)])  53.4 us
    all_gather x1, waiting for transfers between devices, local_heads(): normed_all = lax.all_gather(normed_mid, 'seq', axis=0, tiled=True)  45.4 us
    reduce_scatter x1, waiting for transfers between devices, local_heads(): lax.psum_scatter(mixed, 'seq', scatter_dimension=0, tiled=True).astype(f32)  43.6 us
    dot_general x19, matrix products, dot_across(): lax.dot_general(left_op, right_op, (((0,), (0,)), ((), ())), preferred_el...  35.3 us
    ppermute x24, starting transfers between devices, swap_rows(): return lax.ppermute(block, 'dp', [(i, i ^ hop) for i in range(4)])  28.7 us
    all_to_all x1, waiting for transfers between devices, local_heads(): sent = lax.all_to_all(sent, 'seq', 0, 0, tiled=True)  25.8 us
    all_gather x1, waiting for transfers between devices, local_heads(): cot_all = lax.all_gather(cot_rows, 'seq', axis=0, tiled=True)  25.6 us
    dynamic_update_slice x15, other arithmetic, assemble(): lax.dynamic_update_slice_in_dim(result, block.astype(jnp.float32), start,...  24.8 us
  transfers between devices with their start and end apart: 58, of which 28 were waited for; matrix products, arithmetic and copies ran while one was open for 23% of the time, Pallas kernels for 5%

profile of v3, /device:TPU:0, one launch (start us, length us, event | category | flops | bytes accessed | tf_op | source)
XLA Modules:
  0.0 606.5 jit_solution(3239307751599583001)
XLA Ops:
  18.5 6.3 %all-to-all-start = ((bf16[8,72,384]{2,1,0:T(8,128)(2,1)}), bf16[8,72,384]{2,1,0:T(8,128)(2,1)S(1)}, u32[]{:S(2)}, u32[]{:S(2)}) async-start(bf16[8,72,384]{2,1,0:T(8,128)(2,1)} %pad_maximum_fusion.5), calls=%async_computation | async-start | bytes 884736 | tf_op jit(solution)/shard_map/all_to_all | solution.py:667
  24.9 25.8 %all-to-all-done = bf16[8,72,384]{2,1,0:T(8,128)(2,1)S(1)} async-done(((bf16[8,72,384]{2,1,0:T(8,128)(2,1)}), bf16[8,72,384]{2,1,0:T(8,128)(2,1)S(1)}, u32[]{:S(2)}, u32[]{:S(2)}) %all-to-all-start) | async-done | bytes 442400 | tf_op jit(solution)/shard_map/all_to_all | solution.py:667
  64.9 8.3 %collective-permute-done.1 = bf16[576,384]{1,0:T(8,128)(2,1)} collective-permute-done((bf16[576,384]{1,0:T(8,128)(2,1)S(1)}, bf16[576,384]{1,0:T(8,128)(2,1)}, u32[]{:S(2)}, u32[]{:S(2)}) %collective-permute-start.1) | collective-permute-done | bytes 442400 | tf_op jit(solution)/shard_map/ppermute | solution.py:294
  103.1 9.5 %all-to-all-done.1 = bf16[8,32,512]{2,1,0:T(8,128)(2,1)} async-done(((bf16[8,32,512]{2,1,0:T(8,128)(2,1)}), bf16[8,32,512]{2,1,0:T(8,128)(2,1)}, u32[]{:S(2)}, u32[]{:S(2)}) %all-to-all-start.1) | async-done | bytes 262176 | tf_op jit(solution)/shard_map/all_to_all | solution.py:680
  135.6 12.1 %attend.1 = (bf16[1024,2048]{1,0:T(8,128)(2,1)}, bf16[1024,512]{1,0:T(8,128)(2,1)S(1)}, bf16[1024,512]{1,0:T(8,128)(2,1)S(1)}, bf16[1024,1024]{1,0:T(8,128)(2,1)}) custom-call(bf16[8,1536,128]{2,1,0:T(8,128)(2,1)} %bitcast.237, bf16[8,1536,128]{2,1,0:T(8,128)(2,1)} %bitcast.238, f32[8,128]{1,0:T(8,128)S(1)} %reshape.450.gain_ref, ...), custom_call_target="tpu_custom_call" | custom-call | flops 8000000000 | bytes 16000000 | tf_op jit(solution)/shard_map/attend/pallas_call | solution.py:529
  150.0 25.6 %all-gather.17.cloned.1.call-done = bf16[1,1024,2048]{2,1,0:T(8,128)(2,1)} async-done(((bf16[1,128,2048]{2,1,0:T(8,128)(2,1)}), bf16[1,1024,2048]{2,1,0:T(8,128)(2,1)}) %all-gather.17.cloned.1.call-update) | async-done | bytes 4194320 | tf_op jit(solution)/shard_map/all_gather | solution.py:696
  175.6 7.8 %fusion.5 = f32[1024,704]{0,1:T(8,128)} fusion(bf16[704,2048]{1,0:T(8,128)(2,1)} %param.38, bf16[1,1024,2048]{2,1,0:T(8,128)(2,1)} %all-gather.17.cloned.1.call-done), kind=kOutput, calls=%fused_computation.9 | convolution fusion | flops 2952790016 | bytes 9961472 | tf_op jit(solution)/shard_map/dot_general | solution.py:47
  183.4 43.6 %reduce-scatter.6.cloned.1.call-done = bf16[128,2048]{1,0:T(8,128)(2,1)} async-done(((bf16[1024,2048]{1,0:T(8,128)(2,1)}), bf16[128,2048]{1,0:T(8,128)(2,1)}) %reduce-scatter.6.cloned.1.call-update) | async-done | bytes 524304 | tf_op jit(solution)/shard_map/reduce_scatter | solution.py:721
  230.8 45.4 %all-gather.9.cloned.1.call-done = bf16[1024,2048]{1,0:T(8,128)(2,1)} async-done(((bf16[128,2048]{1,0:T(8,128)(2,1)}), bf16[1024,2048]{1,0:T(8,128)(2,1)}) %all-gather.9.cloned.1.call-update) | async-done | bytes 4194320 | tf_op jit(solution)/shard_map/all_gather | solution.py:729
  276.2 6.0 fusion.101
  282.3 5.4 multiply_convert_fusion
  291.3 5.2 add_convert_fusion
  316.3 11.6 %collective-permute-done.17 = bf16[704,256]{1,0:T(8,128)(2,1)S(1)} collective-permute-done((bf16[704,256]{1,0:T(8,128)(2,1)S(1)}, bf16[704,256]{1,0:T(8,128)(2,1)S(1)}, u32[]{:S(2)}, u32[]{:S(2)}) %collective-permute-start.17) | collective-permute-done | bytes 360480 | tf_op jit(solution)/shard_map/ppermute | solution.py:310
  337.1 5.0 convolution_convert_fusion
  346.5 10.1 %collective-permute-done.12 = bf16[704,256]{1,0:T(8,128)(2,1)} collective-permute-done((bf16[704,256]{1,0:T(8,128)(2,1)}, bf16[704,256]{1,0:T(8,128)(2,1)}, u32[]{:S(2)}, u32[]{:S(2)}) %collective-permute-start.12) | collective-permute-done | bytes 360480 | tf_op jit(solution)/shard_map/ppermute | solution.py:310
  385.7 9.4 %collective-permute-done.19 = bf16[512,704]{0,1:T(8,128)(2,1)S(1)} collective-permute-done((bf16[512,704]{0,1:T(8,128)(2,1)S(1)}, bf16[512,704]{0,1:T(8,128)(2,1)S(1)}, u32[]{:S(2)}, u32[]{:S(2)}) %collective-permute-start.19) | collective-permute-done | bytes 720928 | tf_op jit(solution)/shard_map/ppermute | solution.py:310
  399.7 5.2 all-gather.11.cloned.1.call-done.grad_ref
  417.0 15.7 %attend_back.1 = (bf16[8,1552,128]{2,1,0:T(8,128)(2,1)}, bf16[1024,512]{1,0:T(8,128)(2,1)S(1)}) custom-call(bf16[1024,2048]{1,0:T(8,128)(2,1)} %all-gather.11.cloned.1.call-done.grad_ref, bf16[1024,512]{1,0:T(8,128)(2,1)S(1)} %copy-done.12, bf16[8,1536,128]{2,1,0:T(8,128)(2,1)} %bitcast.239, bf16[8,1536,128]{2,1,0:T(8,128)(2,1)} %bitcast.240, ...), custom_call_target="tpu_custom_call" | custom-call | flops 12000000000 | bytes 20000000 | tf_op jit(solution)/shard_map/attend_back/pallas_call | solution.py:574
  434.2 10.4 %collective-permute-done.24 = bf16[128,2048]{1,0:T(8,128)(2,1)S(1)} collective-permute-done((bf16[128,2048]{1,0:T(8,128)(2,1)S(1)}, bf16[128,2048]{1,0:T(8,128)(2,1)S(1)}, u32[]{:S(2)}, u32[]{:S(2)}) %collective-permute-start.24) | collective-permute-done | bytes 524320 | tf_op jit(solution)/shard_map/ppermute | solution.py:304
  445.9 6.3 %collective-permute-done.28 = bf16[704,256]{1,0:T(8,128)(2,1)S(1)} collective-permute-done((bf16[704,256]{1,0:T(8,128)(2,1)S(1)}, bf16[704,256]{1,0:T(8,128)(2,1)S(1)}, u32[]{:S(2)}, u32[]{:S(2)}) %collective-permute-start.28) | collective-permute-done | bytes 360480 | tf_op jit(solution)/shard_map/ppermute | solution.py:310
  477.3 21.2 %reduce-scatter.12.cloned.1.call-done = bf16[1,1552,128]{2,1,0:T(8,128)(2,1)} async-done(((bf16[8,1552,128]{2,1,0:T(8,128)(2,1)}), bf16[1,1552,128]{2,1,0:T(8,128)(2,1)}) %reduce-scatter.12.cloned.1.call-update) | async-done | bytes 397328 | tf_op jit(solution)/shard_map/reduce_scatter | solution.py:804
  506.3 6.1 %fusion.3 = (bf16[2048]{0:T(1024)(128)(2,1)S(1)}, bf16[1024,2048]{1,0:T(8,128)(2,1)}) fusion(bf16[1,1024,2048]{2,1,0:T(8,128)(2,1)} %all-gather.13.cloned.1.call-done, f32[1024]{0:T(1024)S(1)} %add_rsqrt_fusion.1, bf16[2048,384]{1,0:T(8,128)(2,1)} %bitcast.245, bf16[1024,256]{1,0:T(8,128)(2,1)S(1)} %fusion.77, bf16[1024,128]{1,0:T(8,128)(2,1)S(1)} %get-tuple-element.221), kind=kOutput, calls=%fused_computation.5 | convolution fusion | flops 1622669312 | bytes 10756096 | tf_op jit(solution)/shard_map/dot_general | solution.py:47
  559.0 5.8 collective-permute-done.38
  566.9 6.3 %all-to-all-start.3 = ((bf16[8,72,384]{2,1,0:T(8,128)(2,1)}), bf16[8,72,384]{2,1,0:T(8,128)(2,1)S(1)}, u32[]{:S(2)}, u32[]{:S(2)}) async-start(bf16[8,72,384]{2,1,0:T(8,128)(2,1)} %bitcast.76), calls=%async_computation.8 | async-start | bytes 884736 | tf_op jit(solution)/shard_map/all_to_all | solution.py:864
  (386 shorter events, 276.4 us)
Async XLA Ops:
  7.2 69.1 %all-gather.13.cloned.1.call-start = ((), (), s32[]{:S(2)}) async-start(), calls=%async_computation.16 | async-start | bytes 4718592 | tf_op jit(solution)/shard_map/all_gather | solution.py:676
  18.5 32.2 %all-to-all-start = ((bf16[8,72,384]{2,1,0:T(8,128)(2,1)}), bf16[8,72,384]{2,1,0:T(8,128)(2,1)S(1)}, u32[]{:S(2)}, u32[]{:S(2)}) async-start(bf16[8,72,384]{2,1,0:T(8,128)(2,1)} %pad_maximum_fusion.5), calls=%async_computation | async-start | bytes 884736 | tf_op jit(solution)/shard_map/all_to_all | solution.py:667
  24.8 107.5 %all-gather.15.cloned.1.call-start = ((), (), s32[]{:S(2)}) async-start(), calls=%async_computation.17 | async-start | bytes 3538944 | tf_op jit(solution)/shard_map/all_gather | solution.py:713
  85.6 89.9 %all-gather.17.cloned.1.call-start = ((), (), s32[]{:S(2)}) async-start(), calls=%async_computation.18 | async-start | bytes 4718592 | tf_op jit(solution)/shard_map/all_gather | solution.py:696
  86.5 31.5 %collective-permute-start.7 = (bf16[128,2048]{1,0:T(8,128)(2,1)}, bf16[128,2048]{1,0:T(8,128)(2,1)}, u32[]{:S(2)}, u32[]{:S(2)}) collective-permute-start(bf16[128,2048]{1,0:T(8,128)(2,1)} %param.34), channel_id=1, source_target_pairs={{0,16},{8,24},{16,0},{24,8},{1,17},{9,25},{17,1},{25,9},{2,18},{10... | collective-permute-start | bytes 1572872 | tf_op jit(solution)/shard_map/ppermute | solution.py:294
  88.5 31.4 %collective-permute-start.8 = (bf16[128,2048]{1,0:T(8,128)(2,1)}, bf16[128,2048]{1,0:T(8,128)(2,1)}, u32[]{:S(2)}, u32[]{:S(2)}) collective-permute-start(bf16[128,2048]{1,0:T(8,128)(2,1)} %param.34), channel_id=1, source_target_pairs={{0,24},{8,16},{16,8},{24,0},{1,25},{9,17},{17,9},{25,1},{2,26},{10... | collective-permute-start | bytes 1572872 | tf_op jit(solution)/shard_map/ppermute | solution.py:294
  95.4 131.7 %reduce-scatter.6.cloned.1.call-start = ((), (), s32[]{:S(2)}) async-start(), calls=%async_computation.9 | async-start | bytes 4718592 | tf_op jit(solution)/shard_map/reduce_scatter | solution.py:721
  149.7 126.5 %all-gather.9.cloned.1.call-start = ((), (), s32[]{:S(2)}) async-start(), calls=%async_computation.10 | async-start | bytes 4718592 | tf_op jit(solution)/shard_map/all_gather | solution.py:729
  230.8 114.6 %reduce-scatter.8.cloned.1.call-start = ((), (), s32[]{:S(2)}) async-start(), calls=%async_computation.11 | async-start | bytes 4718592 | tf_op jit(solution)/shard_map/reduce_scatter | solution.py:739
  296.5 108.4 %all-gather.11.cloned.1.call-start = ((), (), s32[]{:S(2)}) async-start(), calls=%async_computation.12 | async-start | bytes 4718592 | tf_op jit(solution)/shard_map/all_gather | solution.py:772
  300.9 55.7 %collective-permute-start.15 = (bf16[512,704]{0,1:T(8,128)(2,1)}, bf16[512,704]{0,1:T(8,128)(2,1)}, u32[]{:S(2)}, u32[]{:S(2)}) collective-permute-start(bf16[512,704]{0,1:T(8,128)(2,1)} %convolution_convert_fusion.4), channel_id=1, source_target_pairs={{0,16},{8,24},{16,0},{24,8},{1,17},{9,25},{17,1},{25,9},{2,18},{10... | collective-permute-start | bytes 2162696 | tf_op jit(solution)/shard_map/ppermute | solution.py:310
  305.4 51.2 %collective-permute-start.14 = (bf16[512,704]{0,1:T(8,128)(2,1)}, bf16[512,704]{0,1:T(8,128)(2,1)}, u32[]{:S(2)}, u32[]{:S(2)}) collective-permute-start(bf16[512,704]{0,1:T(8,128)(2,1)} %convolution_convert_fusion.5), channel_id=1, source_target_pairs={{0,8},{8,0},{16,24},{24,16},{1,9},{9,1},{17,25},{25,17},{2,10},{10... | collective-permute-start | bytes 2162696 | tf_op jit(solution)/shard_map/ppermute | solution.py:310
  359.5 97.0 %reduce-scatter.10.cloned.1.call-start = ((), (), s32[]{:S(2)}) async-start(), calls=%async_computation.13 | async-start | bytes 4718592 | tf_op jit(solution)/shard_map/reduce_scatter | solution.py:775
  404.9 93.6 %reduce-scatter.12.cloned.1.call-start = ((), (), s32[]{:S(2)}) async-start(), calls=%async_computation.14 | async-start | bytes 3575808 | tf_op jit(solution)/shard_map/reduce_scatter | solution.py:804
  410.0 35.9 %collective-permute-start.26 = (bf16[704,256]{1,0:T(8,128)(2,1)}, bf16[704,256]{1,0:T(8,128)(2,1)S(1)}, u32[]{:S(2)}, u32[]{:S(2)}) collective-permute-start(bf16[704,256]{1,0:T(8,128)(2,1)} %add_convert_fusion.7), channel_id=1, source_target_pairs={{0,8},{8,0},{16,24},{24,16},{1,9},{9,1},{17,25},{25,17},{2,10},{10... | collective-permute-start | bytes 1081352 | tf_op jit(solution)/shard_map/ppermute | solution.py:310
  411.5 34.4 %collective-permute-start.27 = (bf16[704,256]{1,0:T(8,128)(2,1)}, bf16[704,256]{1,0:T(8,128)(2,1)}, u32[]{:S(2)}, u32[]{:S(2)}) collective-permute-start(bf16[704,256]{1,0:T(8,128)(2,1)} %add_convert_fusion.7), channel_id=1, source_target_pairs={{0,16},{8,24},{16,0},{24,8},{1,17},{9,25},{17,1},{25,9},{2,18},{10... | collective-permute-start | bytes 1081352 | tf_op jit(solution)/shard_map/ppermute | solution.py:310
  456.5 133.2 %reduce-scatter.14.cloned.1.call-start = ((), (), s32[]{:S(2)}) async-start(), calls=%async_computation.15 | async-start | bytes 4718592 | tf_op jit(solution)/shard_map/reduce_scatter | solution.py:842
  464.1 35.4 %collective-permute-start.33 = (bf16[512,704]{0,1:T(8,128)(2,1)S(1)}, bf16[512,704]{0,1:T(8,128)(2,1)}, u32[]{:S(2)}, u32[]{:S(2)}) collective-permute-start(bf16[512,704]{0,1:T(8,128)(2,1)S(1)} %copy-done.25), channel_id=1, source_target_pairs={{0,8},{8,0},{16,24},{24,16},{1,9},{9,1},{17,25},{25,17},{2,10},{10... | collective-permute-start | bytes 2162696 | tf_op jit(solution)/shard_map/ppermute | solution.py:310
  465.6 33.9 %collective-permute-start.34 = (bf16[512,704]{0,1:T(8,128)(2,1)S(1)}, bf16[512,704]{0,1:T(8,128)(2,1)}, u32[]{:S(2)}, u32[]{:S(2)}) collective-permute-start(bf16[512,704]{0,1:T(8,128)(2,1)S(1)} %copy-done.25), channel_id=1, source_target_pairs={{0,16},{8,24},{16,0},{24,8},{1,17},{9,25},{17,1},{25,9},{2,18},{10... | collective-permute-start | bytes 2162696 | tf_op jit(solution)/shard_map/ppermute | solution.py:310
  469.4 34.5 %collective-permute-start.35 = (bf16[512,704]{0,1:T(8,128)(2,1)S(1)}, bf16[512,704]{0,1:T(8,128)(2,1)}, u32[]{:S(2)}, u32[]{:S(2)}) collective-permute-start(bf16[512,704]{0,1:T(8,128)(2,1)S(1)} %copy-done.24), channel_id=1, source_target_pairs={{0,16},{8,24},{16,0},{24,8},{1,17},{9,25},{17,1},{25,9},{2,18},{10... | collective-permute-start | bytes 2162696 | tf_op jit(solution)/shard_map/ppermute | solution.py:310
  523.5 49.8 %collective-permute-start.43 = (bf16[704,256]{1,0:T(8,128)(2,1)}, bf16[704,256]{1,0:T(8,128)(2,1)}, u32[]{:S(2)}, u32[]{:S(2)}) collective-permute-start(bf16[704,256]{1,0:T(8,128)(2,1)} %collective-permute-done.29), channel_id=1, source_target_pairs={{0,16},{8,24},{16,0},{24,8},{1,17},{9,25},{17,1},{25,9},{2,18},{10... | collective-permute-start | bytes 1081352 | tf_op jit(solution)/shard_map/ppermute | solution.py:310
  524.5 50.6 %collective-permute-start.41 = (bf16[512,704]{0,1:T(8,128)(2,1)}, bf16[512,704]{0,1:T(8,128)(2,1)}, u32[]{:S(2)}, u32[]{:S(2)}) collective-permute-start(bf16[512,704]{0,1:T(8,128)(2,1)} %collective-permute-done.36), channel_id=1, source_target_pairs={{0,16},{8,24},{16,0},{24,8},{1,17},{9,25},{17,1},{25,9},{2,18},{10... | collective-permute-start | bytes 2162696 | tf_op jit(solution)/shard_map/ppermute | solution.py:310
  534.3 30.6 %collective-permute-start.38 = (bf16[576,384]{1,0:T(8,128)(2,1)}, bf16[576,384]{1,0:T(8,128)(2,1)S(1)}, u32[]{:S(2)}, u32[]{:S(2)}) collective-permute-start(bf16[576,384]{1,0:T(8,128)(2,1)} %get-tuple-element.231), channel_id=1, source_target_pairs={{0,16},{8,24},{16,0},{24,8},{1,17},{9,25},{17,1},{25,9},{2,18},{10... | collective-permute-start | bytes 1327112 | tf_op jit(solution)/shard_map/ppermute | solution.py:304
  535.7 30.6 %all-to-all-start.2 = ((bf16[8,32,512]{2,1,0:T(8,128)(2,1)}), bf16[8,32,512]{2,1,0:T(8,128)(2,1)S(1)}, u32[]{:S(2)}, u32[]{:S(2)}) async-start(bf16[8,32,512]{2,1,0:T(8,128)(2,1)} %bitcast.74), calls=%async_computation.7 | async-start | bytes 524288 | tf_op jit(solution)/shard_map/all_to_all | solution.py:859
  (90 other events, 1262.0 us)
Sparse Core Ops, SparseCore 0:
  9.6 59.2 all-gather.12
  85.8 42.1 all-gather.14
  129.6 45.9 all-gather.16
  178.3 48.7 reduce-scatter.5
  230.9 45.2 all-gather.8
  296.6 48.7 reduce-scatter.7
  359.6 45.2 all-gather.10
  407.7 48.7 reduce-scatter.9
  459.4 39.0 reduce-scatter.11
  512.6 53.8 reduce-scatter.13
